TPU v7x, 32 devices: a whole 2x2x4 slice. The times are simulated.
32 devices in a mesh: section: 2 (over x), rows: 4 (over y, core), cols: 4 (over z).
Axes of the slice: x: 2, y: 2, z: 4, core: 2. Of those that a mesh axis runs over, the one named last changes fastest.
Arguments:
- features: bfloat16 [2, 96, 96, 728], P(None, ('rows', 'cols')), may hold values from -6 to 6
- upstream: bfloat16 [2, 96, 96, 256], P(None, 'rows', 'cols'), may hold values from -0.046875 to 0.046875
- depth_mid: float32 [9, 728], replicated, may hold values from -2 to 2
- point_mid: bfloat16 [728, 728], replicated, may hold values from -0.21875 to 0.21875
- projection: bfloat16 [728, 2048], replicated, may hold values from -0.21875 to 0.21875
- depth_first: float32 [9, 2048], replicated, may hold values from -2 to 2
- point_first: bfloat16 [2048, 256], replicated, may hold values from -0.125 to 0.125
- depth_later: float32 [2, 9, 256], replicated, may hold values from -2 to 2
- point_later: bfloat16 [2, 256, 256], replicated, may hold values from -0.375 to 0.375
- joining: bfloat16 [768, 256], replicated, may hold values from -0.21875 to 0.21875
- rate_first: int32 [2], replicated, may hold values from 1 to 6, as said below
- rates_later: int32 [2, 2], replicated, may hold values from 1 to 21, as said below
Outputs:
- grad_mid: float32 [728, 728], replicated
- grad_later: float32 [2, 256, 256], replicated
Inputs may be any that keep to these rules, and one draw needn't show every extreme that they name: `rate_first`: at least one of the two rates equals 6. `rates_later`: at least one of the rates equals 21.
All inputs are finite; a program needn't handle non-finite values.
Results may differ from a plain program's by a relative error of at most 0.015.
Values may be sent and summed in bfloat16 or wider, within the bound.
A program may use at most 128 MiB of HBM per device.

v0:
```python
import jax
import jax.numpy as jnp
from jax import lax
from jax.sharding import PartitionSpec as P

LATER = 2
R0 = 6
RMAX = 21


def as_sent(value):
    return jax.tree.map(lambda a: a.astype(jnp.bfloat16) if a.dtype == jnp.float32 else a, value)


def with_halo(cells, sides, width):
    for axis, dim in sides:
        count = lax.axis_size(axis)
        ends = count - 1
        head = lax.slice_in_dim(cells, 0, width, axis=dim)
        tail = lax.slice_in_dim(cells, cells.shape[dim] - width, cells.shape[dim], axis=dim)
        cells = jnp.concatenate(
            [
                lax.ppermute(tail, axis, [(i, (i + 1) % count) for i in range(ends)]),
                cells,
                lax.ppermute(head, axis, [((i + 1) % count, i) for i in range(ends)]),
            ],
            axis=dim,
        )
    return cells


def from_partner(value, axis, distance):
    return lax.ppermute(value, axis, [(i, i ^ 1 << distance) for i in range(lax.axis_size(axis))])


def silu_slope(argument):
    sigmoid_value = jax.nn.sigmoid(argument)
    return sigmoid_value * (1.0 + argument * (1.0 - sigmoid_value))


def dilated(padded, weights, rates_pair, margin, height, breadth, direction):
    depth = padded.shape[2]
    summed = jnp.zeros((height, breadth, depth), jnp.float32)
    for row_step in (-1, 0, 1):
        for col_step in (-1, 0, 1):
            row_start = margin + direction * row_step * rates_pair[0]
            col_start = margin + direction * col_step * rates_pair[1]
            window = lax.dynamic_slice(
                padded, (row_start, col_start, jnp.zeros((), jnp.int32)), (height, breadth, depth)
            )
            summed = (
                summed + window.astype(jnp.float32) * weights[3 * (row_step + 1) + col_step + 1]
            )
    return summed


def section_only(active, compute, *operands):

    def resting(*inputs):
        return jax.tree.map(jnp.zeros_like, compute(*inputs))

    return lax.cond(active, compute, resting, *operands)


def extend_tile(field, margin):
    return with_halo(as_sent(field), (("rows", 0), ("cols", 1)), margin).astype(field.dtype)


def backbone_local(haloed, features_now, depth_mid, point_mid):
    activated = jax.nn.silu(haloed.astype(jnp.float32))
    padded = jnp.pad(activated, ((0, 0), (1, 1), (0, 0)))
    unit_rates = jnp.ones((2,), jnp.int32)
    height, breadth = (features_now.shape[0], features_now.shape[1])
    mid_conv = dilated(padded, depth_mid, unit_rates, 1, height, breadth, 1).astype(jnp.bfloat16)
    mixed = jnp.einsum("hwc,cd->hwd", mid_conv, point_mid, preferred_element_type=jnp.float32)
    section_out = (features_now.astype(jnp.float32) + mixed).astype(jnp.bfloat16)
    return (section_out, mid_conv)


def mid_gradient(mid_conv, section_back):
    return jnp.einsum("hwc,hwd->cd", mid_conv, section_back, preferred_element_type=jnp.float32)


def project(field, projection):
    return jnp.einsum("hwc,ck->hwk", field, projection, preferred_element_type=jnp.float32).astype(
        jnp.bfloat16
    )


def head_front(padded_proj, depth_first, point_first, rate_first):
    height = padded_proj.shape[0] - 2 * R0
    breadth = padded_proj.shape[1] - 2 * R0
    first_conv = dilated(padded_proj, depth_first, rate_first, R0, height, breadth, 1).astype(
        jnp.bfloat16
    )
    first_pre = jnp.einsum(
        "hwc,cd->hwd", first_conv, point_first, preferred_element_type=jnp.float32
    )
    return (jax.nn.silu(first_pre).astype(jnp.bfloat16), first_pre)


def head_middle(padded_first, upstream_now, depth_later, point_later, rates_later, joining):
    height, breadth, channels = upstream_now.shape
    upstream_back = jnp.einsum(
        "hwb,kb->hwk", upstream_now, joining, preferred_element_type=jnp.float32
    )
    branch_backs = []
    branch_grads = []
    for branch in range(LATER):
        later_conv = dilated(
            padded_first, depth_later[branch], rates_later[branch], RMAX, height, breadth, 1
        ).astype(jnp.bfloat16)
        later_pre = jnp.einsum(
            "hwc,cd->hwd", later_conv, point_later[branch], preferred_element_type=jnp.float32
        )
        block = upstream_back[:, :, (branch + 1) * channels : (branch + 2) * channels]
        later_gate = (block * silu_slope(later_pre)).astype(jnp.bfloat16)
        later_back = jnp.einsum(
            "hwd,cd->hwc", later_gate, point_later[branch], preferred_element_type=jnp.float32
        )
        branch_backs.append(later_back.astype(jnp.bfloat16))
        branch_grads.append(
            jnp.einsum("hwc,hwd->cd", later_conv, later_gate, preferred_element_type=jnp.float32)
        )
    return (
        jnp.concatenate(branch_backs, axis=2),
        jnp.stack(branch_grads),
        upstream_back[:, :, :channels],
    )


def head_back(padded_backs, first_direct, first_pre, depth_later, rates_later, point_first):
    height, breadth, channels = first_direct.shape
    first_back = first_direct
    for branch in range(LATER):
        portion = padded_backs[:, :, branch * channels : (branch + 1) * channels]
        first_back = first_back + dilated(
            portion, depth_later[branch], rates_later[branch], RMAX, height, breadth, -1
        )
    first_gate = (first_back * silu_slope(first_pre)).astype(jnp.bfloat16)
    conv_back = jnp.einsum(
        "hwd,cd->hwc", first_gate, point_first, preferred_element_type=jnp.float32
    )
    return conv_back.astype(jnp.bfloat16)


def head_end(padded_conv, depth_first, rate_first, projection):
    height = padded_conv.shape[0] - 2 * R0
    breadth = padded_conv.shape[1] - 2 * R0
    projected_back = dilated(padded_conv, depth_first, rate_first, R0, height, breadth, -1).astype(
        jnp.bfloat16
    )
    section_back = jnp.einsum(
        "hwk,ck->hwc", projected_back, projection, preferred_element_type=jnp.float32
    )
    return section_back.astype(jnp.bfloat16)


def head_pass(
    act_tile,
    upstream_now,
    trailing,
    projection,
    depth_first,
    point_first,
    depth_later,
    point_later,
    joining,
    rate_first,
    rates_later,
):
    padded_features = extend_tile(act_tile, R0)
    padded_proj = section_only(trailing, project, padded_features, projection)
    first_out, first_pre = section_only(
        trailing, head_front, padded_proj, depth_first, point_first, rate_first
    )
    padded_first = extend_tile(first_out, RMAX)
    branch_backs, later_terms, first_direct = section_only(
        trailing,
        head_middle,
        padded_first,
        upstream_now,
        depth_later,
        point_later,
        rates_later,
        joining,
    )
    padded_backs = extend_tile(branch_backs, RMAX)
    conv_back = section_only(
        trailing,
        head_back,
        padded_backs,
        first_direct,
        first_pre,
        depth_later,
        rates_later,
        point_first,
    )
    padded_conv = extend_tile(conv_back, R0)
    section_back = section_only(
        trailing, head_end, padded_conv, depth_first, rate_first, projection
    )
    return (section_back, later_terms)


def local(
    features,
    upstream,
    depth_mid,
    point_mid,
    projection,
    depth_first,
    point_first,
    depth_later,
    point_later,
    joining,
    rate_first,
    rates_later,
):
    groups = lax.axis_size("cols")
    leading = lax.axis_index("section") == 0
    trailing = jnp.logical_not(leading)
    micro_count, slab_rows, full_width, channels_mid = features.shape
    tile_rows = slab_rows * groups
    tile_cols = full_width // groups
    channels_head = point_later.shape[1]
    received = jnp.zeros((slab_rows, full_width, channels_mid), jnp.bfloat16)
    saved_convs = []
    grad_mid = jnp.zeros((channels_mid, channels_mid), jnp.float32)
    grad_later = jnp.zeros((LATER, channels_head, channels_head), jnp.float32)
    for moment in range(micro_count + 1):
        if moment < micro_count:
            haloed = with_halo(features[moment], ((("rows", "cols"), 0),), 1)
            section_out, mid_conv = section_only(
                leading, backbone_local, haloed, features[moment], depth_mid, point_mid
            )
            saved_convs.append(mid_conv)
        else:
            section_out = jnp.zeros((slab_rows, full_width, channels_mid), jnp.bfloat16)
        if moment > 0:
            act_tile = received.reshape(slab_rows, groups, tile_cols, channels_mid).transpose(
                1, 0, 2, 3
            )
            act_tile = act_tile.reshape(tile_rows, tile_cols, channels_mid)
            section_back, later_terms = head_pass(
                act_tile,
                upstream[moment - 1],
                trailing,
                projection,
                depth_first,
                point_first,
                depth_later,
                point_later,
                joining,
                rate_first,
                rates_later,
            )
            grad_later = grad_later + later_terms
        else:
            section_back = jnp.zeros((tile_rows, tile_cols, channels_mid), jnp.bfloat16)
        slab_message = section_out.reshape(slab_rows, groups, tile_cols, channels_mid).transpose(
            1, 0, 2, 3
        )
        tile_message = section_back.reshape(groups, slab_rows, tile_cols, channels_mid)
        message = jnp.where(leading, slab_message, tile_message)
        regrouped = lax.all_to_all(
            message, "cols", split_axis=0, concat_axis=2, tiled=True
        ).reshape(slab_rows, full_width, channels_mid)
        received = from_partner(regrouped, "section", 0)
        if moment > 0:
            grad_mid = grad_mid + section_only(
                leading, mid_gradient, saved_convs[moment - 1], received
            )
    grad_mid, grad_later = lax.psum((grad_mid, grad_later), ("section", "rows", "cols"))
    return (grad_mid, grad_later)


def solution(mesh):
    placed = (
        P(None, ("rows", "cols"), None, None),
        P(None, "rows", "cols", None),
        P(),
        P(),
        P(),
        P(),
        P(),
        P(),
        P(),
        P(),
        P(),
        P(),
    )
    return jax.shard_map(local, mesh=mesh, in_specs=placed, out_specs=(P(), P()), check_vma=False)
```

profile of v0, /device:TPU:0, one launch (start us, length us, event | category | flops | bytes accessed | tf_op | source)
XLA Modules:
  0.0 804.4 jit_solution(9014674131988072642)
XLA Ops:
  23.2 6.9 collective-permute-done.3
  31.4 6.9 conditional.14
  38.4 25.0 %all_to_all.45 = bf16[4,6,24,728]{3,2,1,0:T(8,128)(2,1)S(1)} all-to-all(bf16[4,6,24,728]{3,2,1,0:T(8,128)(2,1)S(1)} %copy.107), channel_id=1, replica_groups=mesh['section'=2,'rows'=4,'cols'=4] {'cols'}, dimensions={0} | all-to-all | bytes 1677312 | tf_op jit(solution)/shard_map/all_to_all | solution.py:266
  63.6 22.4 %collective-permute-done.4 = bf16[6,96,728]{2,1,0:T(8,128)(2,1)S(1)} collective-permute-done((bf16[6,96,728]{2,1,0:T(8,128)(2,1)S(1)}, bf16[6,96,728]{2,1,0:T(8,128)(2,1)S(1)}, u32[]{:S(2)}, u32[]{:S(2)}) %collective-permute-start.4) | collective-permute-done | bytes 838688 | tf_op jit(solution)/shard_map/ppermute | solution.py:33
  94.8 6.2 collective-permute-done.7
  124.0 12.6 %collective-permute-done.11 = bf16[66,21,256]{2,0,1:T(8,128)(2,1)S(1)} collective-permute-done((bf16[66,21,256]{2,0,1:T(8,128)(2,1)S(1)}, bf16[66,21,256]{2,0,1:T(8,128)(2,1)S(1)}, u32[]{:S(2)}, u32[]{:S(2)}) %collective-permute-start.11) | collective-permute-done | bytes 709664 | tf_op jit(solution)/shard_map/ppermute | solution.py:23
  158.5 26.8 %collective-permute-done.15 = bf16[66,21,512]{2,0,1:T(8,128)(2,1)S(1)} collective-permute-done((bf16[66,21,512]{2,0,1:T(8,128)(2,1)S(1)}, bf16[66,21,512]{2,0,1:T(8,128)(2,1)S(1)}, u32[]{:S(2)}, u32[]{:S(2)}) %collective-permute-start.15) | collective-permute-done | bytes 1419296 | tf_op jit(solution)/shard_map/ppermute | solution.py:23
  190.1 6.0 pad_maximum_fusion.6
  196.5 7.5 collective-permute-start.17
  221.2 8.8 %collective-permute-done.19 = bf16[36,6,2048]{2,0,1:T(8,128)(2,1)} collective-permute-done((bf16[36,6,2048]{2,0,1:T(8,128)(2,1)}, bf16[36,6,2048]{2,0,1:T(8,128)(2,1)}, u32[]{:S(2)}, u32[]{:S(2)}) %collective-permute-start.19) | collective-permute-done | bytes 884768 | tf_op jit(solution)/shard_map/ppermute | solution.py:23
  243.3 24.0 %all_to_all.46 = bf16[4,6,24,728]{3,2,1,0:T(8,128)(2,1)S(1)} all-to-all(bf16[4,6,24,728]{3,2,1,0:T(8,128)(2,1)S(1)} %copy.125), channel_id=1, replica_groups=mesh['section'=2,'rows'=4,'cols'=4] {'cols'}, dimensions={0} | all-to-all | bytes 1677312 | tf_op jit(solution)/shard_map/all_to_all | solution.py:266
  267.4 82.6 %collective-permute-start.21 = (bf16[6,96,728]{2,1,0:T(8,128)(2,1)S(1)}, bf16[6,96,728]{2,1,0:T(8,128)(2,1)S(1)}, u32[]{:S(2)}, u32[]{:S(2)}) collective-permute-start(bf16[6,96,728]{2,1,0:T(8,128)(2,1)S(1)} %bitcast.382), channel_id=1, source_target_pairs={{0,16},{16,0},{1,17},{17,1},{2,18},{18,2},{3,19},{19,3},{4,20},{20... | collective-permute-start | bytes 2515976 | tf_op jit(solution)/shard_map/ppermute | solution.py:33
  350.0 19.3 %collective-permute-done.21 = bf16[6,96,728]{2,1,0:T(8,128)(2,1)S(1)} collective-permute-done((bf16[6,96,728]{2,1,0:T(8,128)(2,1)S(1)}, bf16[6,96,728]{2,1,0:T(8,128)(2,1)S(1)}, u32[]{:S(2)}, u32[]{:S(2)}) %collective-permute-start.21) | collective-permute-done | bytes 838688 | tf_op jit(solution)/shard_map/ppermute | solution.py:33
  379.1 6.2 collective-permute-done.24
  407.3 12.6 %collective-permute-done.28 = bf16[66,21,256]{2,0,1:T(8,128)(2,1)S(1)} collective-permute-done((bf16[66,21,256]{2,0,1:T(8,128)(2,1)S(1)}, bf16[66,21,256]{2,0,1:T(8,128)(2,1)S(1)}, u32[]{:S(2)}, u32[]{:S(2)}) %collective-permute-start.28) | collective-permute-done | bytes 709664 | tf_op jit(solution)/shard_map/ppermute | solution.py:23
  442.4 26.8 %collective-permute-done.32 = bf16[66,21,512]{2,0,1:T(8,128)(2,1)S(1)} collective-permute-done((bf16[66,21,512]{2,0,1:T(8,128)(2,1)S(1)}, bf16[66,21,512]{2,0,1:T(8,128)(2,1)S(1)}, u32[]{:S(2)}, u32[]{:S(2)}) %collective-permute-start.32) | collective-permute-done | bytes 1419296 | tf_op jit(solution)/shard_map/ppermute | solution.py:23
  474.0 6.0 pad_maximum_fusion.7
  480.9 7.5 collective-permute-start.34
  496.5 14.1 %collective-permute-done.36 = bf16[36,6,2048]{2,0,1:T(8,128)(2,1)S(1)} collective-permute-done((bf16[36,6,2048]{2,0,1:T(8,128)(2,1)S(1)}, bf16[36,6,2048]{2,0,1:T(8,128)(2,1)S(1)}, u32[]{:S(2)}, u32[]{:S(2)}) %collective-permute-start.36) | collective-permute-done | bytes 884768 | tf_op jit(solution)/shard_map/ppermute | solution.py:23
  515.4 8.9 %pad_maximum_fusion.5 = bf16[36,36,2048]{2,0,1:T(8,128)(2,1)} fusion(bf16[36,6,2048]{2,0,1:T(8,128)(2,1)S(1)} %collective-permute-done.37, bf16[6,24,2048]{2,0,1:T(8,128)(2,1)S(1)} %copy.140, bf16[24,24,2048]{2,0,1:T(8,128)(2,1)S(1)} %copy.139, bf16[6,24,2048]{2,0,1:T(8,128)(2,1)S(1)} %copy.138, bf16[36,6,2048]{2,0,1:T(8,128)(2,1)S(1)} %collective-permute-done.36), kind=kLoop, calls=%fused_computation.195 | loop fusion | flops 26542080 | bytes 10616832 | tf_op jit(solution)/shard_map/concatenate | solution.py:21
  524.6 23.7 %all_to_all.47 = bf16[4,6,24,728]{3,2,1,0:T(8,128)(2,1)S(1)} all-to-all(bf16[4,6,24,728]{3,2,1,0:T(8,128)(2,1)S(1)} %copy.143), channel_id=1, replica_groups=mesh['section'=2,'rows'=4,'cols'=4] {'cols'}, dimensions={0} | all-to-all | bytes 1677312 | tf_op jit(solution)/shard_map/all_to_all | solution.py:266
  549.4 82.7 %collective-permute-start.38 = (bf16[6,96,728]{2,1,0:T(8,128)(2,1)}, bf16[6,96,728]{2,1,0:T(8,128)(2,1)}, u32[]{:S(2)}, u32[]{:S(2)}) collective-permute-start(bf16[6,96,728]{2,1,0:T(8,128)(2,1)} %bitcast.268), channel_id=1, source_target_pairs={{0,16},{16,0},{1,17},{17,1},{2,18},{18,2},{3,19},{19,3},{4,20},{20... | collective-permute-start | bytes 2515976 | tf_op jit(solution)/shard_map/ppermute | solution.py:33
  636.4 14.9 %collective-permute-done.38 = bf16[6,96,728]{2,1,0:T(8,128)(2,1)} collective-permute-done((bf16[6,96,728]{2,1,0:T(8,128)(2,1)}, bf16[6,96,728]{2,1,0:T(8,128)(2,1)}, u32[]{:S(2)}, u32[]{:S(2)}) %collective-permute-start.38) | collective-permute-done | bytes 838688 | tf_op jit(solution)/shard_map/ppermute | solution.py:33
  658.5 134.9 %all-reduce.5.cloned.1.call-done = (f32[728,728]{1,0:T(8,128)}, f32[2,256,256]{2,1,0:T(8,128)}) async-done(((f32[728,728]{1,0:T(8,128)}, f32[2,256,256]{2,1,0:T(8,128)}), (f32[728,728]{1,0:T(8,128)}, f32[2,256,256]{2,1,0:T(8,128)})) %all-reduce.5.cloned.1.call-update) | async-done | bytes 2644240 | tf_op jit(solution)/shard_map/psum | solution.py:274
  (204 shorter events, 226.2 us)
Async XLA Ops:
  7.2 786.2 %all-reduce.5.cloned.1.call-start = ((), (), s32[]{:S(2)}) async-start(), calls=%async_computation.3 | async-start | bytes 5521408 | tf_op jit(solution)/shard_map/psum | solution.py:274
  8.4 13.7 %collective-permute-start.2 = (bf16[1,96,728]{2,1,0:T(8,128)(2,1)S(1)}, bf16[1,96,728]{2,1,0:T(8,128)(2,1)S(1)}, u32[]{:S(2)}, u32[]{:S(2)}) collective-permute-start(bf16[1,96,728]{2,1,0:T(8,128)(2,1)S(1)} %get-tuple-element.600), channel_id=1, source_target_pairs={{0,1},{1,2},{2,3},{3,4},{4,5},{5,6},{6,7},{7,8},{8,9},{9,10},{10,1... | collective-permute-start | bytes 419336 | tf_op jit(solution)/shard_map/ppermute | solution.py:23
  13.3 9.9 %collective-permute-start.1 = (bf16[1,96,728]{2,1,0:T(8,128)(2,1)S(1)}, bf16[1,96,728]{2,1,0:T(8,128)(2,1)S(1)}, u32[]{:S(2)}, u32[]{:S(2)}) collective-permute-start(bf16[1,96,728]{2,1,0:T(8,128)(2,1)S(1)} %get-tuple-element.601), channel_id=1, source_target_pairs={{1,0},{2,1},{3,2},{4,3},{5,4},{6,5},{7,6},{8,7},{9,8},{10,9},{11,1... | collective-permute-start | bytes 419336 | tf_op jit(solution)/shard_map/ppermute | solution.py:25
  19.2 10.9 %collective-permute-start.3 = (bf16[1,96,728]{2,1,0:T(8,128)(2,1)S(1)}, bf16[1,96,728]{2,1,0:T(8,128)(2,1)S(1)}, u32[]{:S(2)}, u32[]{:S(2)}) collective-permute-start(bf16[1,96,728]{2,1,0:T(8,128)(2,1)S(1)} %get-tuple-element.603), channel_id=1, source_target_pairs={{1,0},{2,1},{3,2},{4,3},{5,4},{6,5},{7,6},{8,7},{9,8},{10,9},{11,1... | collective-permute-start | bytes 419336 | tf_op jit(solution)/shard_map/ppermute | solution.py:25
  63.5 22.5 %collective-permute-start.4 = (bf16[6,96,728]{2,1,0:T(8,128)(2,1)S(1)}, bf16[6,96,728]{2,1,0:T(8,128)(2,1)S(1)}, u32[]{:S(2)}, u32[]{:S(2)}) collective-permute-start(bf16[6,96,728]{2,1,0:T(8,128)(2,1)S(1)} %bitcast.381), channel_id=1, source_target_pairs={{0,16},{16,0},{1,17},{17,1},{2,18},{18,2},{3,19},{19,3},{4,20},{20... | collective-permute-start | bytes 2515976 | tf_op jit(solution)/shard_map/ppermute | solution.py:33
  93.5 12.3 %collective-permute-start.8 = (bf16[36,6,728]{2,1,0:T(8,128)(2,1)S(1)}, bf16[36,6,728]{2,1,0:T(8,128)(2,1)}, u32[]{:S(2)}, u32[]{:S(2)}) collective-permute-start(bf16[36,6,728]{2,1,0:T(8,128)(2,1)S(1)} %get-tuple-element.609), channel_id=1, source_target_pairs={{1,0},{2,1},{3,2},{5,4},{6,5},{7,6},{9,8},{10,9},{11,10},{13,12},{... | collective-permute-start | bytes 943496 | tf_op jit(solution)/shard_map/ppermute | solution.py:25
  120.3 16.3 %collective-permute-start.11 = (bf16[66,21,256]{2,0,1:T(8,128)(2,1)S(1)}, bf16[66,21,256]{2,0,1:T(8,128)(2,1)S(1)}, u32[]{:S(2)}, u32[]{:S(2)}) collective-permute-start(bf16[66,21,256]{2,0,1:T(8,128)(2,1)S(1)} %get-tuple-element.614), channel_id=1, source_target_pairs={{0,1},{1,2},{2,3},{4,5},{5,6},{6,7},{8,9},{9,10},{10,11},{12,13},{... | collective-permute-start | bytes 2128904 | tf_op jit(solution)/shard_map/ppermute | solution.py:23
  122.7 18.7 %collective-permute-start.12 = (bf16[66,21,256]{2,0,1:T(8,128)(2,1)S(1)}, bf16[66,21,256]{2,0,1:T(8,128)(2,1)S(1)}, u32[]{:S(2)}, u32[]{:S(2)}) collective-permute-start(bf16[66,21,256]{2,0,1:T(8,128)(2,1)S(1)} %get-tuple-element.615), channel_id=1, source_target_pairs={{1,0},{2,1},{3,2},{5,4},{6,5},{7,6},{9,8},{10,9},{11,10},{13,12},{... | collective-permute-start | bytes 2128904 | tf_op jit(solution)/shard_map/ppermute | solution.py:25
  153.7 31.5 %collective-permute-start.15 = (bf16[66,21,512]{2,0,1:T(8,128)(2,1)S(1)}, bf16[66,21,512]{2,0,1:T(8,128)(2,1)S(1)}, u32[]{:S(2)}, u32[]{:S(2)}) collective-permute-start(bf16[66,21,512]{2,0,1:T(8,128)(2,1)S(1)} %get-tuple-element.598), channel_id=1, source_target_pairs={{0,1},{1,2},{2,3},{4,5},{5,6},{6,7},{8,9},{9,10},{10,11},{12,13},{... | collective-permute-start | bytes 4257800 | tf_op jit(solution)/shard_map/ppermute | solution.py:23
  157.1 32.9 %collective-permute-start.16 = (bf16[66,21,512]{2,0,1:T(8,128)(2,1)S(1)}, bf16[66,21,512]{2,0,1:T(8,128)(2,1)S(1)}, u32[]{:S(2)}, u32[]{:S(2)}) collective-permute-start(bf16[66,21,512]{2,0,1:T(8,128)(2,1)S(1)} %get-tuple-element.599), channel_id=1, source_target_pairs={{1,0},{2,1},{3,2},{5,4},{6,5},{7,6},{9,8},{10,9},{11,10},{13,12},{... | collective-permute-start | bytes 4257800 | tf_op jit(solution)/shard_map/ppermute | solution.py:25
  196.5 11.9 %collective-permute-start.17 = (bf16[6,24,2048]{2,1,0:T(8,128)(2,1)S(1)}, bf16[6,24,2048]{2,1,0:T(8,128)(2,1)S(1)}, u32[]{:S(2)}, u32[]{:S(2)}) collective-permute-start(bf16[6,24,2048]{2,1,0:T(8,128)(2,1)S(1)} %get-tuple-element.594), channel_id=1, source_target_pairs={{0,4},{4,8},{8,12},{1,5},{5,9},{9,13},{2,6},{6,10},{10,14},{3,7},{... | collective-permute-start | bytes 1769480 | tf_op jit(solution)/shard_map/ppermute | solution.py:23
  211.2 18.8 %collective-permute-start.19 = (bf16[36,6,2048]{2,0,1:T(8,128)(2,1)}, bf16[36,6,2048]{2,0,1:T(8,128)(2,1)}, u32[]{:S(2)}, u32[]{:S(2)}) collective-permute-start(bf16[36,6,2048]{2,0,1:T(8,128)(2,1)} %get-tuple-element.590), channel_id=1, source_target_pairs={{0,1},{1,2},{2,3},{4,5},{5,6},{6,7},{8,9},{9,10},{10,11},{12,13},{... | collective-permute-start | bytes 2654216 | tf_op jit(solution)/shard_map/ppermute | solution.py:23
  214.0 21.6 %collective-permute-start.20 = (bf16[36,6,2048]{2,0,1:T(8,128)(2,1)}, bf16[36,6,2048]{2,0,1:T(8,128)(2,1)}, u32[]{:S(2)}, u32[]{:S(2)}) collective-permute-start(bf16[36,6,2048]{2,0,1:T(8,128)(2,1)} %get-tuple-element.591), channel_id=1, source_target_pairs={{1,0},{2,1},{3,2},{5,4},{6,5},{7,6},{9,8},{10,9},{11,10},{13,12},{... | collective-permute-start | bytes 2654216 | tf_op jit(solution)/shard_map/ppermute | solution.py:25
  267.4 102.0 %collective-permute-start.21 = (bf16[6,96,728]{2,1,0:T(8,128)(2,1)S(1)}, bf16[6,96,728]{2,1,0:T(8,128)(2,1)S(1)}, u32[]{:S(2)}, u32[]{:S(2)}) collective-permute-start(bf16[6,96,728]{2,1,0:T(8,128)(2,1)S(1)} %bitcast.382), channel_id=1, source_target_pairs={{0,16},{16,0},{1,17},{17,1},{2,18},{18,2},{3,19},{19,3},{4,20},{20... | collective-permute-start | bytes 2515976 | tf_op jit(solution)/shard_map/ppermute | solution.py:33
  375.8 9.5 %collective-permute-start.24 = (bf16[36,6,728]{2,1,0:T(8,128)(2,1)S(1)}, bf16[36,6,728]{2,1,0:T(8,128)(2,1)S(1)}, u32[]{:S(2)}, u32[]{:S(2)}) collective-permute-start(bf16[36,6,728]{2,1,0:T(8,128)(2,1)S(1)} %get-tuple-element.606), channel_id=1, source_target_pairs={{0,1},{1,2},{2,3},{4,5},{5,6},{6,7},{8,9},{9,10},{10,11},{12,13},{... | collective-permute-start | bytes 943496 | tf_op jit(solution)/shard_map/ppermute | solution.py:23
  377.8 12.2 %collective-permute-start.25 = (bf16[36,6,728]{2,1,0:T(8,128)(2,1)S(1)}, bf16[36,6,728]{2,1,0:T(8,128)(2,1)S(1)}, u32[]{:S(2)}, u32[]{:S(2)}) collective-permute-start(bf16[36,6,728]{2,1,0:T(8,128)(2,1)S(1)} %get-tuple-element.607), channel_id=1, source_target_pairs={{1,0},{2,1},{3,2},{5,4},{6,5},{7,6},{9,8},{10,9},{11,10},{13,12},{... | collective-permute-start | bytes 943496 | tf_op jit(solution)/shard_map/ppermute | solution.py:25
  403.1 16.8 %collective-permute-start.28 = (bf16[66,21,256]{2,0,1:T(8,128)(2,1)S(1)}, bf16[66,21,256]{2,0,1:T(8,128)(2,1)S(1)}, u32[]{:S(2)}, u32[]{:S(2)}) collective-permute-start(bf16[66,21,256]{2,0,1:T(8,128)(2,1)S(1)} %get-tuple-element.610), channel_id=1, source_target_pairs={{0,1},{1,2},{2,3},{4,5},{5,6},{6,7},{8,9},{9,10},{10,11},{12,13},{... | collective-permute-start | bytes 2128904 | tf_op jit(solution)/shard_map/ppermute | solution.py:23
  406.0 18.5 %collective-permute-start.29 = (bf16[66,21,256]{2,0,1:T(8,128)(2,1)S(1)}, bf16[66,21,256]{2,0,1:T(8,128)(2,1)S(1)}, u32[]{:S(2)}, u32[]{:S(2)}) collective-permute-start(bf16[66,21,256]{2,0,1:T(8,128)(2,1)S(1)} %get-tuple-element.611), channel_id=1, source_target_pairs={{1,0},{2,1},{3,2},{5,4},{6,5},{7,6},{9,8},{10,9},{11,10},{13,12},{... | collective-permute-start | bytes 2128904 | tf_op jit(solution)/shard_map/ppermute | solution.py:25
  437.2 32.1 %collective-permute-start.32 = (bf16[66,21,512]{2,0,1:T(8,128)(2,1)S(1)}, bf16[66,21,512]{2,0,1:T(8,128)(2,1)S(1)}, u32[]{:S(2)}, u32[]{:S(2)}) collective-permute-start(bf16[66,21,512]{2,0,1:T(8,128)(2,1)S(1)} %get-tuple-element.596), channel_id=1, source_target_pairs={{0,1},{1,2},{2,3},{4,5},{5,6},{6,7},{8,9},{9,10},{10,11},{12,13},{... | collective-permute-start | bytes 4257800 | tf_op jit(solution)/shard_map/ppermute | solution.py:23
  441.1 32.9 %collective-permute-start.33 = (bf16[66,21,512]{2,0,1:T(8,128)(2,1)S(1)}, bf16[66,21,512]{2,0,1:T(8,128)(2,1)S(1)}, u32[]{:S(2)}, u32[]{:S(2)}) collective-permute-start(bf16[66,21,512]{2,0,1:T(8,128)(2,1)S(1)} %get-tuple-element.597), channel_id=1, source_target_pairs={{1,0},{2,1},{3,2},{5,4},{6,5},{7,6},{9,8},{10,9},{11,10},{13,12},{... | collective-permute-start | bytes 4257800 | tf_op jit(solution)/shard_map/ppermute | solution.py:25
  480.9 10.1 %collective-permute-start.34 = (bf16[6,24,2048]{2,1,0:T(8,128)(2,1)S(1)}, bf16[6,24,2048]{2,1,0:T(8,128)(2,1)S(1)}, u32[]{:S(2)}, u32[]{:S(2)}) collective-permute-start(bf16[6,24,2048]{2,1,0:T(8,128)(2,1)S(1)} %get-tuple-element.592), channel_id=1, source_target_pairs={{0,4},{4,8},{8,12},{1,5},{5,9},{9,13},{2,6},{6,10},{10,14},{3,7},{... | collective-permute-start | bytes 1769480 | tf_op jit(solution)/shard_map/ppermute | solution.py:23
  493.3 17.3 %collective-permute-start.36 = (bf16[36,6,2048]{2,0,1:T(8,128)(2,1)S(1)}, bf16[36,6,2048]{2,0,1:T(8,128)(2,1)S(1)}, u32[]{:S(2)}, u32[]{:S(2)}) collective-permute-start(bf16[36,6,2048]{2,0,1:T(8,128)(2,1)S(1)} %get-tuple-element.588), channel_id=1, source_target_pairs={{0,1},{1,2},{2,3},{4,5},{5,6},{6,7},{8,9},{9,10},{10,11},{12,13},{... | collective-permute-start | bytes 2654216 | tf_op jit(solution)/shard_map/ppermute | solution.py:23
  495.2 20.1 %collective-permute-start.37 = (bf16[36,6,2048]{2,0,1:T(8,128)(2,1)S(1)}, bf16[36,6,2048]{2,0,1:T(8,128)(2,1)S(1)}, u32[]{:S(2)}, u32[]{:S(2)}) collective-permute-start(bf16[36,6,2048]{2,0,1:T(8,128)(2,1)S(1)} %get-tuple-element.589), channel_id=1, source_target_pairs={{1,0},{2,1},{3,2},{5,4},{6,5},{7,6},{9,8},{10,9},{11,10},{13,12},{... | collective-permute-start | bytes 2654216 | tf_op jit(solution)/shard_map/ppermute | solution.py:25
  549.4 101.9 %collective-permute-start.38 = (bf16[6,96,728]{2,1,0:T(8,128)(2,1)}, bf16[6,96,728]{2,1,0:T(8,128)(2,1)}, u32[]{:S(2)}, u32[]{:S(2)}) collective-permute-start(bf16[6,96,728]{2,1,0:T(8,128)(2,1)} %bitcast.268), channel_id=1, source_target_pairs={{0,16},{16,0},{1,17},{17,1},{2,18},{18,2},{3,19},{19,3},{4,20},{20... | collective-permute-start | bytes 2515976 | tf_op jit(solution)/shard_map/ppermute | solution.py:33
  (38 other events, 409.1 us)
Sparse Core Ops, SparseCore 0:
  658.6 134.7 all-reduce.4
where the time goes:
time: 813 us; the launch traced here: 804 us
  waiting for transfers between devices  365 us (45%)
  starting transfers between devices  259 us (32%)
  blocking collectives  72.7 us (9%)
  other arithmetic  50.5 us (6%)
  local copies, waits for them, and re-layouts  30.2 us (4%)
  between operations  15.2 us (2%)
  matrix products  10.2 us (1%)
    ppermute x3, starting transfers between devices, from_partner(): lax.ppermute(value, axis, [(i, i ^ 1 << distance) for i in range(lax.axis...  165 us
    psum x1, waiting for transfers between devices, local(): lax.psum((grad_mid, grad_later), ('section', 'rows', 'cols'))  135 us
    ppermute x18, waiting for transfers between devices, with_halo(): lax.ppermute(tail, axis, [(i, (i + 1) % count) for i in range(ends)])  114 us
    all_to_all x3, blocking collectives, local(): lax.all_to_all(message, 'cols', split_axis=0, concat_axis=2, tiled=True)  72.7 us
    ppermute x18, starting transfers between devices, with_halo(): lax.ppermute(tail, axis, [(i, (i + 1) % count) for i in range(ends)])  69.8 us
    ppermute x18, waiting for transfers between devices, with_halo(): lax.ppermute(head, axis, [((i + 1) % count, i) for i in range(ends)])  58.9 us
    ppermute x3, waiting for transfers between devices, from_partner(): lax.ppermute(value, axis, [(i, i ^ 1 << distance) for i in range(lax.axis...  56.6 us
    concatenate x13, other arithmetic, with_halo(): jnp.concatenate([lax.ppermute(tail, axis, [(i, (i + 1) % count) for i in...  34.5 us
  transfers between devices with their start and end apart: 40, of which 29 were waited for; matrix products, arithmetic and copies ran while one was open for 2% of the time, Pallas kernels for 0%

commit v1 on v0

v1 whole, which is shorter than its diff:
```python
import jax
import jax.numpy as jnp
from jax import lax
from jax.sharding import PartitionSpec as P

LATER = 2
R0 = 6
RMAX = 21


def as_sent(value):
    return jax.tree.map(lambda a: a.astype(jnp.bfloat16) if a.dtype == jnp.float32 else a, value)


def with_halo(cells, sides, width):
    for axis, dim in sides:
        count = lax.axis_size(axis)
        ends = count - 1
        head = lax.slice_in_dim(cells, 0, width, axis=dim)
        tail = lax.slice_in_dim(cells, cells.shape[dim] - width, cells.shape[dim], axis=dim)
        cells = jnp.concatenate(
            [
                lax.ppermute(tail, axis, [(i, (i + 1) % count) for i in range(ends)]),
                cells,
                lax.ppermute(head, axis, [((i + 1) % count, i) for i in range(ends)]),
            ],
            axis=dim,
        )
    return cells


def silu_slope(argument):
    sigmoid_value = jax.nn.sigmoid(argument)
    return sigmoid_value * (1.0 + argument * (1.0 - sigmoid_value))


def dilated(padded, weights, rates_pair, margin, height, breadth, direction):
    depth = padded.shape[2]
    summed = jnp.zeros((height, breadth, depth), jnp.float32)
    for row_step in (-1, 0, 1):
        for col_step in (-1, 0, 1):
            row_start = margin + direction * row_step * rates_pair[0]
            col_start = margin + direction * col_step * rates_pair[1]
            window = lax.dynamic_slice(
                padded, (row_start, col_start, jnp.zeros((), jnp.int32)), (height, breadth, depth)
            )
            summed = (
                summed + window.astype(jnp.float32) * weights[3 * (row_step + 1) + col_step + 1]
            )
    return summed


def extend_tile(field, margin):
    return with_halo(as_sent(field), (("cols", 1), ("rows", 0)), margin).astype(field.dtype)


def backbone_local(haloed, features_now, depth_mid, point_mid):
    activated = jax.nn.silu(haloed.astype(jnp.float32))
    height, breadth, depth = features_now.shape
    mid_conv = jnp.zeros((height, breadth, depth), jnp.float32)
    for row in range(3):
        for col in range(3):
            mid_conv = (
                mid_conv
                + activated[row : row + height, col : col + breadth] * depth_mid[3 * row + col]
            )
    mid_conv = mid_conv.astype(jnp.bfloat16)
    mixed = jnp.einsum("hwc,cd->hwd", mid_conv, point_mid, preferred_element_type=jnp.float32)
    section_out = (features_now.astype(jnp.float32) + mixed).astype(jnp.bfloat16)
    return (section_out, mid_conv)


def mid_gradient(mid_conv, section_back):
    return jnp.einsum("hwc,hwd->cd", mid_conv, section_back, preferred_element_type=jnp.float32)


def project(field, projection):
    return jnp.einsum("hwc,ck->hwk", field, projection, preferred_element_type=jnp.float32).astype(
        jnp.bfloat16
    )


def head_front(padded_proj, depth_first, point_first, rate_first):
    height = padded_proj.shape[0] - 2 * R0
    breadth = padded_proj.shape[1] - 2 * R0
    first_conv = dilated(padded_proj, depth_first, rate_first, R0, height, breadth, 1).astype(
        jnp.bfloat16
    )
    first_pre = jnp.einsum(
        "hwc,cd->hwd", first_conv, point_first, preferred_element_type=jnp.float32
    )
    return (jax.nn.silu(first_pre).astype(jnp.bfloat16), first_pre)


def head_middle(padded_first, upstream_now, depth_later, point_later, rates_later, joining):
    height, breadth, channels = upstream_now.shape
    upstream_back = jnp.einsum(
        "hwb,kb->hwk", upstream_now, joining, preferred_element_type=jnp.float32
    )
    branch_backs = []
    branch_grads = []
    for branch in range(LATER):
        later_conv = dilated(
            padded_first, depth_later[branch], rates_later[branch], RMAX, height, breadth, 1
        ).astype(jnp.bfloat16)
        later_pre = jnp.einsum(
            "hwc,cd->hwd", later_conv, point_later[branch], preferred_element_type=jnp.float32
        )
        block = upstream_back[:, :, (branch + 1) * channels : (branch + 2) * channels]
        later_gate = (block * silu_slope(later_pre)).astype(jnp.bfloat16)
        later_back = jnp.einsum(
            "hwd,cd->hwc", later_gate, point_later[branch], preferred_element_type=jnp.float32
        )
        branch_backs.append(later_back.astype(jnp.bfloat16))
        branch_grads.append(
            jnp.einsum("hwc,hwd->cd", later_conv, later_gate, preferred_element_type=jnp.float32)
        )
    return (
        jnp.concatenate(branch_backs, axis=2),
        jnp.stack(branch_grads),
        upstream_back[:, :, :channels],
    )


def head_back(padded_backs, first_direct, first_pre, depth_later, rates_later):
    height, breadth, channels = first_direct.shape
    first_back = first_direct
    for branch in range(LATER):
        portion = padded_backs[:, :, branch * channels : (branch + 1) * channels]
        first_back = first_back + dilated(
            portion, depth_later[branch], rates_later[branch], RMAX, height, breadth, -1
        )
    return (first_back * silu_slope(first_pre)).astype(jnp.bfloat16)


def conv_gradient(padded_gate, point_first):
    return jnp.einsum(
        "hwd,cd->hwc", padded_gate, point_first, preferred_element_type=jnp.float32
    ).astype(jnp.bfloat16)


def head_end(padded_conv, depth_first, rate_first, projection):
    height = padded_conv.shape[0] - 2 * R0
    breadth = padded_conv.shape[1] - 2 * R0
    projected_back = dilated(padded_conv, depth_first, rate_first, R0, height, breadth, -1).astype(
        jnp.bfloat16
    )
    section_back = jnp.einsum(
        "hwk,ck->hwc", projected_back, projection, preferred_element_type=jnp.float32
    )
    return section_back.astype(jnp.bfloat16)


def local(
    features,
    upstream,
    depth_mid,
    point_mid,
    projection,
    depth_first,
    point_first,
    depth_later,
    point_later,
    joining,
    rate_first,
    rates_later,
):
    sections = lax.axis_size("section")
    section = lax.axis_index("section")
    micro_count = features.shape[0]
    channels_mid = features.shape[3]
    channels_head = point_later.shape[1]
    grad_mid = jnp.zeros((channels_mid, channels_mid), jnp.float32)
    grad_later = jnp.zeros((LATER, channels_head, channels_head), jnp.float32)
    for turn in range(micro_count // sections):
        micro = turn * sections + section
        slab = lax.dynamic_index_in_dim(features, micro, 0, keepdims=False)
        upstream_now = lax.dynamic_index_in_dim(upstream, micro, 0, keepdims=False)
        tile = lax.all_to_all(slab, "cols", split_axis=1, concat_axis=0, tiled=True)
        section_out, mid_conv = backbone_local(extend_tile(tile, 1), tile, depth_mid, point_mid)
        padded_proj = project(extend_tile(section_out, R0), projection)
        first_out, first_pre = head_front(padded_proj, depth_first, point_first, rate_first)
        branch_backs, later_terms, first_direct = head_middle(
            extend_tile(first_out, RMAX),
            upstream_now,
            depth_later,
            point_later,
            rates_later,
            joining,
        )
        first_gate = head_back(
            extend_tile(branch_backs, RMAX), first_direct, first_pre, depth_later, rates_later
        )
        padded_conv = conv_gradient(extend_tile(first_gate, R0), point_first)
        section_back = head_end(padded_conv, depth_first, rate_first, projection)
        grad_mid = grad_mid + mid_gradient(mid_conv, section_back)
        grad_later = grad_later + later_terms
    grad_later = lax.psum(grad_later, ("section", "rows", "cols"))
    grad_mid = lax.psum(grad_mid, ("section", "rows", "cols"))
    return (grad_mid, grad_later)


def solution(mesh):
    placed = (
        P(None, ("rows", "cols"), None, None),
        P(None, "rows", "cols", None),
        P(),
        P(),
        P(),
        P(),
        P(),
        P(),
        P(),
        P(),
        P(),
        P(),
    )
    return jax.shard_map(local, mesh=mesh, in_specs=placed, out_specs=(P(), P()), check_vma=False)
```

time: 813 us -> 388 us (0.48)
  starting transfers between devices: 259 us -> 63.6 us
  waiting for transfers between devices: 365 us -> 180 us
  matrix products: 10.2 us -> 48.4 us
  blocking collectives: 72.7 us -> 34.8 us
  other arithmetic: 50.5 us -> 18.1 us
  local copies, waits for them, and re-layouts: 30.2 us -> 12.7 us
  between operations: 15.2 us -> 26.2 us
    ppermute x3 -> x0, starting transfers between devices: 165 us -> none  [from_partner(): lax.ppermute(value, axis, [(i, i ^ 1 << distance) for i in range(lax.axis...]
    ppermute x18 -> x10, waiting for transfers between devices: 114 us -> 7.2 us  [with_halo(): lax.ppermute(tail, axis, [(i, (i + 1) % count) for i in range(ends)])]
    ppermute x3 -> x0, waiting for transfers between devices: 56.6 us -> none  [from_partner(): lax.ppermute(value, axis, [(i, i ^ 1 << distance) for i in range(lax.axis...]
    all_to_all x3 -> x1, blocking collectives: 72.7 us -> 34.8 us  [local(): tile = lax.all_to_all(slab, 'cols', split_axis=1, concat_axis=0, tiled=True)]
    concatenate x13 -> x4, other arithmetic: 34.5 us -> 7.85 us  [with_halo(): jnp.concatenate([lax.ppermute(tail, axis, [(i, (i + 1) % count) for i in...]
    dot_general x0 -> x10, matrix products: none -> 24.5 us  [the longest x1 10.4 us: head_front(): jnp.einsum('hwc,cd->hwd', first_conv, point_first, preferred_element_type...]
    ppermute x18 -> x10, waiting for transfers between devices: 58.9 us -> 35.7 us  [with_halo(): lax.ppermute(head, axis, [((i + 1) % count, i) for i in range(ends)])]
    ppermute x18 -> x10, starting transfers between devices: 69.8 us -> 50 us  [with_halo(): lax.ppermute(tail, axis, [(i, (i + 1) % count) for i in range(ends)])]
  transfers between devices with their start and end apart: 40 -> 21, of which waited for: 29 -> 15; matrix products, arithmetic and copies ran while one was open for 2% -> 1% of each run, Pallas kernels for 0% -> 0%
where the time goes in v1:
time: 388 us; the launch traced here: 383 us
  waiting for transfers between devices  180 us (46%)
  starting transfers between devices  63.6 us (16%)
  matrix products  48.4 us (12%)
  blocking collectives  34.8 us (9%)
  between operations  26.2 us (7%)
  other arithmetic  18.1 us (5%)
  local copies, waits for them, and re-layouts  12.7 us (3%)
    psum x1, waiting for transfers between devices, local(): grad_mid = lax.psum(grad_mid, ('section', 'rows', 'cols'))  137 us
    ppermute x10, starting transfers between devices, with_halo(): lax.ppermute(tail, axis, [(i, (i + 1) % count) for i in range(ends)])  50 us
    ppermute x10, waiting for transfers between devices, with_halo(): lax.ppermute(head, axis, [((i + 1) % count, i) for i in range(ends)])  35.7 us
    all_to_all x1, blocking collectives, local(): tile = lax.all_to_all(slab, 'cols', split_axis=1, concat_axis=0, tiled=True)  34.8 us
    dot_general x1, matrix products, mid_gradient(): jnp.einsum('hwc,hwd->cd', mid_conv, section_back, preferred_element_type=...  23 us
    ppermute x10, starting transfers between devices, with_halo(): lax.ppermute(head, axis, [((i + 1) % count, i) for i in range(ends)])  13.5 us
    dot_general x1, matrix products, head_front(): jnp.einsum('hwc,cd->hwd', first_conv, point_first, preferred_element_type...  10.4 us
    concatenate x4, other arithmetic, with_halo(): jnp.concatenate([lax.ppermute(tail, axis, [(i, (i + 1) % count) for i in...  7.85 us
  transfers between devices with their start and end apart: 21, of which 15 were waited for; matrix products, arithmetic and copies ran while one was open for 1% of the time, Pallas kernels for 0%

profile of v1, /device:TPU:0, one launch (start us, length us, event | category | flops | bytes accessed | tf_op | source)
XLA Modules:
  0.0 383.3 jit_solution(15859973524539555967)
XLA Ops:
  9.1 34.8 %all_to_all.18 = bf16[6,96,728]{2,0,1:T(8,128)(2,1)S(1)} all-to-all(bf16[6,96,728]{2,0,1:T(8,128)(2,1)S(1)} %bitcast.117), channel_id=1, replica_groups=mesh['section'=2,'rows'=4,'cols'=4] {'cols'}, dimensions={1} | all-to-all | bytes 1677312 | tf_op jit(solution)/shard_map/all_to_all | solution.py:179
  48.3 4.3 %collective-permute-done.1 = bf16[24,1,728]{2,1,0:T(2,128)(2,1)S(1)} collective-permute-done((bf16[24,1,728]{2,1,0:T(2,128)(2,1)S(1)}, bf16[24,1,728]{2,1,0:T(2,128)(2,1)S(1)}, u32[]{:S(2)}, u32[]{:S(2)}) %collective-permute-start.1) | collective-permute-done | bytes 34976 | tf_op jit(solution)/shard_map/ppermute | solution.py:25
  55.3 3.5 collective-permute-done.3
  64.2 2.5 collective-permute-start.4
  72.6 4.6 %collective-permute-done.5 = bf16[24,6,728]{2,1,0:T(8,128)(2,1)} collective-permute-done((bf16[24,6,728]{2,1,0:T(8,128)(2,1)}, bf16[24,6,728]{2,1,0:T(8,128)(2,1)}, u32[]{:S(2)}, u32[]{:S(2)}) %collective-permute-start.5) | collective-permute-done | bytes 209696 | tf_op jit(solution)/shard_map/ppermute | solution.py:25
  78.5 3.4 collective-permute-start.6
  85.5 6.3 %convolution_convert_fusion = bf16[36,36,2048]{2,1,0:T(8,128)(2,1)S(1)} fusion(bf16[728,2048]{1,0:T(8,128)(2,1)S(1)} %copy-done, bf16[6,36,728]{2,1,0:T(8,128)(2,1)S(1)} %collective-permute-done.7, bf16[24,6,728]{2,1,0:T(8,128)(2,1)} %collective-permute-done.5, bf16[24,24,728]{2,1,0:T(8,128)(2,1)} %copy-done.1, ...), kind=kOutput, calls=%fused_computation.3 | convolution fusion | flops 3876615936 | bytes 10177280 | tf_op jit(solution)/shard_map/hwc,ck->hwk/dot_general | solution.py:78
  91.9 10.4 %multiply_convert_fusion = (bf16[24,24,256]{2,1,0:T(8,128)(2,1)S(1)}, f32[24,24,256]{2,1,0:T(8,128)}) fusion(bf16[2048,256]{1,0:T(8,128)(2,1)S(1)} %copy-done.16, bf16[36,36,2048]{2,1,0:T(8,128)(2,1)S(1)} %convolution_convert_fusion, f32[2048]{0:T(1024)S(1)} %bitcast.169, s32[]{:T(128)S(6)} %select_n.34, s32[]{:T(128)S(6)} %select_n.33, ...), kind=kOutput, calls=%fused_computation.88 | convolution fusion | flops 636567552 | bytes 23240720 | tf_op jit(solution)/shard_map/hwc,cd->hwd/dot_general | solution.py:89
  102.4 3.7 collective-permute-start.8
  107.4 2.9 collective-permute-done.8
  110.3 4.4 %collective-permute-done.9 = bf16[24,21,256]{2,1,0:T(8,128)(2,1)S(1)} collective-permute-done((bf16[24,21,256]{2,1,0:T(8,128)(2,1)S(1)}, bf16[24,21,256]{2,1,0:T(8,128)(2,1)S(1)}, u32[]{:S(2)}, u32[]{:S(2)}) %collective-permute-start.9) | collective-permute-done | bytes 258080 | tf_op jit(solution)/shard_map/ppermute | solution.py:25
  116.3 6.6 %collective-permute-start.10 = (bf16[21,66,256]{2,1,0:T(8,128)(2,1)}, bf16[21,66,256]{2,1,0:T(8,128)(2,1)}, u32[]{:S(2)}, u32[]{:S(2)}) collective-permute-start(bf16[21,66,256]{2,1,0:T(8,128)(2,1)} %get-tuple-element.21), channel_id=1, source_target_pairs={{0,4},{4,8},{8,12},{1,5},{5,9},{9,13},{2,6},{6,10},{10,14},{3,7},{... | collective-permute-start | bytes 2128904 | tf_op jit(solution)/shard_map/ppermute | solution.py:23
  141.4 4.6 %collective-permute-start.12 = (bf16[24,21,512]{2,0,1:T(8,128)(2,1)S(1)}, bf16[24,21,512]{2,0,1:T(8,128)(2,1)S(1)}, u32[]{:S(2)}, u32[]{:S(2)}) collective-permute-start(bf16[24,21,512]{2,0,1:T(8,128)(2,1)S(1)} %copy.18), channel_id=1, source_target_pairs={{0,1},{1,2},{2,3},{4,5},{5,6},{6,7},{8,9},{9,10},{10,11},{12,13},{... | collective-permute-start | bytes 1548296 | tf_op jit(solution)/shard_map/ppermute | solution.py:23
  146.0 8.5 %collective-permute-done.13 = bf16[24,21,512]{2,0,1:T(8,128)(2,1)S(1)} collective-permute-done((bf16[24,21,512]{2,0,1:T(8,128)(2,1)S(1)}, bf16[24,21,512]{2,0,1:T(8,128)(2,1)S(1)}, u32[]{:S(2)}, u32[]{:S(2)}) %collective-permute-start.13) | collective-permute-done | bytes 516128 | tf_op jit(solution)/shard_map/ppermute | solution.py:25
  157.4 3.8 collective-permute-start.14
  164.1 2.8 collective-permute-done.15
  166.9 5.3 %pad_maximum_fusion = bf16[66,66,512]{2,1,0:T(8,128)(2,1)S(1)} fusion(bf16[21,66,512]{2,1,0:T(8,128)(2,1)S(1)} %collective-permute-done.15, bf16[24,21,512]{2,1,0:T(8,128)(2,1)S(1)} %copy.21, bf16[24,24,256]{2,1,0:T(8,128)(2,1)S(1)} %convolution_convert_fusion.2, bf16[24,24,256]{2,1,0:T(8,128)(2,1)S(1)} %convolution_convert_fusion.3, ...), kind=kLoop, calls=%fused_computation | loop fusion | flops 26763264 | bytes 8921088 | tf_op jit(solution)/shard_map/concatenate | solution.py:21
  175.7 4.5 %collective-permute-start.16 = (bf16[24,6,256]{2,1,0:T(8,128)(2,1)S(1)}, bf16[24,6,256]{2,1,0:T(8,128)(2,1)S(1)}, u32[]{:S(2)}, u32[]{:S(2)}) collective-permute-start(bf16[24,6,256]{2,1,0:T(8,128)(2,1)S(1)} %get-tuple-element.31), channel_id=1, source_target_pairs={{0,1},{1,2},{2,3},{4,5},{5,6},{6,7},{8,9},{9,10},{10,11},{12,13},{... | collective-permute-start | bytes 221192 | tf_op jit(solution)/shard_map/ppermute | solution.py:23
  182.5 4.3 %collective-permute-done.17 = bf16[24,6,256]{2,1,0:T(8,128)(2,1)S(1)} collective-permute-done((bf16[24,6,256]{2,1,0:T(8,128)(2,1)S(1)}, bf16[24,6,256]{2,1,0:T(8,128)(2,1)S(1)}, u32[]{:S(2)}, u32[]{:S(2)}) %collective-permute-start.17) | collective-permute-done | bytes 73760 | tf_op jit(solution)/shard_map/ppermute | solution.py:25
  186.9 17.5 %collective-permute-start.18 = (bf16[6,36,256]{2,1,0:T(8,128)(2,1)S(1)}, bf16[6,36,256]{2,1,0:T(8,128)(2,1)S(1)}, u32[]{:S(2)}, u32[]{:S(2)}) collective-permute-start(bf16[6,36,256]{2,1,0:T(8,128)(2,1)S(1)} %get-tuple-element.29), channel_id=1, source_target_pairs={{0,4},{4,8},{8,12},{1,5},{5,9},{9,13},{2,6},{6,10},{10,14},{3,7},{... | collective-permute-start | bytes 331784 | tf_op jit(solution)/shard_map/ppermute | solution.py:23
  208.1 4.3 %convolution_convert_fusion.1 = bf16[36,36,2048]{2,1,0:T(8,128)(2,1)} fusion(bf16[2048,256]{1,0:T(8,128)(2,1)S(1)} %copy-done.17, bf16[6,36,256]{2,1,0:T(8,128)(2,1)S(1)} %collective-permute-done.19, bf16[24,6,256]{2,1,0:T(8,128)(2,1)S(1)} %collective-permute-done.17, bf16[24,24,256]{2,1,0:T(8,128)(2,1)S(1)} %fusion.58, ...), kind=kOutput, calls=%fused_computation.4 | convolution fusion | flops 1364926464 | bytes 7020544 | tf_op jit(solution)/shard_map/hwd,cd->hwc/dot_general | solution.py:137
  212.4 23.0 %convolution_bitcast_fusion = f32[728,728]{1,0:T(8,128)} fusion(bf16[24,24,728]{2,1,0:T(8,128)(2,1)} %copy-done.6, bf16[728,2048]{1,0:T(8,128)(2,1)S(1)} %copy-done, bf16[36,36,2048]{2,1,0:T(8,128)(2,1)} %convolution_convert_fusion.1, s32[]{:T(128)S(6)} %select_n.31, s32[]{:T(128)S(6)} %select_n.32, s32[]{:T(128)S(6)} %select_n.33, s32[]{:T(128)S(6)} %select_n.34, ...), kind=kOutput, calls=%fused_computation.44 | convolution fusion | flops 2360378880 | bytes 27293968 | tf_op jit(solution)/shard_map/hwc,hwd->cd/dot_general | solution.py:74
  235.4 136.7 %all-reduce.3.cloned.1.call-done = (f32[728,728]{1,0:T(8,128)}, f32[2,256,256]{2,1,0:T(8,128)}) async-done(((f32[728,728]{1,0:T(8,128)}, f32[2,256,256]{2,1,0:T(8,128)}), (f32[728,728]{1,0:T(8,128)}, f32[2,256,256]{2,1,0:T(8,128)})) %all-reduce.3.cloned.1.call-update) | async-done | bytes 2644240 | tf_op jit(solution)/shard_map/psum | solution.py:199
  372.0 3.2 copy.27
  (103 shorter events, 51.3 us)
Async XLA Ops:
  7.2 78.3 %copy-start = (bf16[728,2048]{1,0:T(8,128)(2,1)S(1)}, bf16[728,2048]{1,0:T(8,128)(2,1)}, u32[]{:S(2)}) copy-start(bf16[728,2048]{1,0:T(8,128)(2,1)} %param.16) | copy-start | bytes 8945668
  7.2 364.8 %all-reduce.3.cloned.1.call-start = ((), (), s32[]{:S(2)}) async-start(), calls=%async_computation.1 | async-start | bytes 5521408 | tf_op jit(solution)/shard_map/psum | solution.py:199
  9.1 46.1 %copy-start.12 = (f32[9,728]{1,0:T(8,128)S(1)}, f32[9,728]{1,0:T(8,128)}, u32[]{:S(2)}) copy-start(f32[9,728]{1,0:T(8,128)} %param.14) | copy-start | bytes 78628
  44.2 4.1 %collective-permute-start = (bf16[24,1,728]{2,1,0:T(2,128)(2,1)S(1)}, bf16[24,1,728]{2,1,0:T(2,128)(2,1)S(1)}, u32[]{:S(2)}, u32[]{:S(2)}) collective-permute-start(bf16[24,1,728]{2,1,0:T(2,128)(2,1)S(1)} %get-tuple-element.25), channel_id=1, source_target_pairs={{0,1},{1,2},{2,3},{4,5},{5,6},{6,7},{8,9},{9,10},{10,11},{12,13},{... | collective-permute-start | bytes 104840 | tf_op jit(solution)/shard_map/ppermute | solution.py:23
  46.3 6.2 %collective-permute-start.1 = (bf16[24,1,728]{2,1,0:T(2,128)(2,1)S(1)}, bf16[24,1,728]{2,1,0:T(2,128)(2,1)S(1)}, u32[]{:S(2)}, u32[]{:S(2)}) collective-permute-start(bf16[24,1,728]{2,1,0:T(2,128)(2,1)S(1)} %get-tuple-element.26), channel_id=1, source_target_pairs={{1,0},{2,1},{3,2},{5,4},{6,5},{7,6},{9,8},{10,9},{11,10},{13,12},{... | collective-permute-start | bytes 104840 | tf_op jit(solution)/shard_map/ppermute | solution.py:25
  52.6 2.7 collective-permute-start.2
  53.9 4.9 %collective-permute-start.3 = (bf16[1,26,728]{2,1,0:T(8,128)(2,1)S(1)}, bf16[1,26,728]{2,1,0:T(8,128)(2,1)S(1)}, u32[]{:S(2)}, u32[]{:S(2)}) collective-permute-start(bf16[1,26,728]{2,1,0:T(8,128)(2,1)S(1)} %get-tuple-element.20), channel_id=1, source_target_pairs={{4,0},{8,4},{12,8},{5,1},{9,5},{13,9},{6,2},{10,6},{14,10},{7,3},{... | collective-permute-start | bytes 113576 | tf_op jit(solution)/shard_map/ppermute | solution.py:25
  64.2 8.3 %collective-permute-start.4 = (bf16[24,6,728]{2,1,0:T(8,128)(2,1)}, bf16[24,6,728]{2,1,0:T(8,128)(2,1)S(1)}, u32[]{:S(2)}, u32[]{:S(2)}) collective-permute-start(bf16[24,6,728]{2,1,0:T(8,128)(2,1)} %get-tuple-element.23), channel_id=1, source_target_pairs={{0,1},{1,2},{2,3},{4,5},{5,6},{6,7},{8,9},{9,10},{10,11},{12,13},{... | collective-permute-start | bytes 629000 | tf_op jit(solution)/shard_map/ppermute | solution.py:23
  66.7 10.4 %collective-permute-start.5 = (bf16[24,6,728]{2,1,0:T(8,128)(2,1)}, bf16[24,6,728]{2,1,0:T(8,128)(2,1)}, u32[]{:S(2)}, u32[]{:S(2)}) collective-permute-start(bf16[24,6,728]{2,1,0:T(8,128)(2,1)} %get-tuple-element.24), channel_id=1, source_target_pairs={{1,0},{2,1},{3,2},{5,4},{6,5},{7,6},{9,8},{10,9},{11,10},{13,12},{... | collective-permute-start | bytes 629000 | tf_op jit(solution)/shard_map/ppermute | solution.py:25
  78.5 5.0 %collective-permute-start.6 = (bf16[6,36,728]{2,1,0:T(8,128)(2,1)S(1)}, bf16[6,36,728]{2,1,0:T(8,128)(2,1)S(1)}, u32[]{:S(2)}, u32[]{:S(2)}) collective-permute-start(bf16[6,36,728]{2,1,0:T(8,128)(2,1)S(1)} %get-tuple-element.17), channel_id=1, source_target_pairs={{0,4},{4,8},{8,12},{1,5},{5,9},{9,13},{2,6},{6,10},{10,14},{3,7},{... | collective-permute-start | bytes 943496 | tf_op jit(solution)/shard_map/ppermute | solution.py:23
  81.9 3.6 collective-permute-start.7
  102.4 7.9 %collective-permute-start.8 = (bf16[24,21,256]{2,1,0:T(8,128)(2,1)S(1)}, bf16[24,21,256]{2,1,0:T(8,128)(2,1)S(1)}, u32[]{:S(2)}, u32[]{:S(2)}) collective-permute-start(bf16[24,21,256]{2,1,0:T(8,128)(2,1)S(1)} %get-tuple-element.33), channel_id=1, source_target_pairs={{0,1},{1,2},{2,3},{4,5},{5,6},{6,7},{8,9},{9,10},{10,11},{12,13},{... | collective-permute-start | bytes 774152 | tf_op jit(solution)/shard_map/ppermute | solution.py:23
  106.1 8.6 %collective-permute-start.9 = (bf16[24,21,256]{2,1,0:T(8,128)(2,1)S(1)}, bf16[24,21,256]{2,1,0:T(8,128)(2,1)S(1)}, u32[]{:S(2)}, u32[]{:S(2)}) collective-permute-start(bf16[24,21,256]{2,1,0:T(8,128)(2,1)S(1)} %get-tuple-element.34), channel_id=1, source_target_pairs={{1,0},{2,1},{3,2},{5,4},{6,5},{7,6},{9,8},{10,9},{11,10},{13,12},{... | collective-permute-start | bytes 774152 | tf_op jit(solution)/shard_map/ppermute | solution.py:25
  116.3 17.6 %collective-permute-start.10 = (bf16[21,66,256]{2,1,0:T(8,128)(2,1)}, bf16[21,66,256]{2,1,0:T(8,128)(2,1)}, u32[]{:S(2)}, u32[]{:S(2)}) collective-permute-start(bf16[21,66,256]{2,1,0:T(8,128)(2,1)} %get-tuple-element.21), channel_id=1, source_target_pairs={{0,4},{4,8},{8,12},{1,5},{5,9},{9,13},{2,6},{6,10},{10,14},{3,7},{... | collective-permute-start | bytes 2128904 | tf_op jit(solution)/shard_map/ppermute | solution.py:23
  122.9 11.0 %collective-permute-start.11 = (bf16[21,66,256]{2,1,0:T(8,128)(2,1)}, bf16[21,66,256]{2,1,0:T(8,128)(2,1)}, u32[]{:S(2)}, u32[]{:S(2)}) collective-permute-start(bf16[21,66,256]{2,1,0:T(8,128)(2,1)} %get-tuple-element.22), channel_id=1, source_target_pairs={{4,0},{8,4},{12,8},{5,1},{9,5},{13,9},{6,2},{10,6},{14,10},{7,3},{... | collective-permute-start | bytes 2128904 | tf_op jit(solution)/shard_map/ppermute | solution.py:25
  139.9 14.6 %collective-permute-start.13 = (bf16[24,21,512]{2,0,1:T(8,128)(2,1)S(1)}, bf16[24,21,512]{2,0,1:T(8,128)(2,1)S(1)}, u32[]{:S(2)}, u32[]{:S(2)}) collective-permute-start(bf16[24,21,512]{2,0,1:T(8,128)(2,1)S(1)} %copy.19), channel_id=1, source_target_pairs={{1,0},{2,1},{3,2},{5,4},{6,5},{7,6},{9,8},{10,9},{11,10},{13,12},{... | collective-permute-start | bytes 1548296 | tf_op jit(solution)/shard_map/ppermute | solution.py:25
  141.4 15.0 %collective-permute-start.12 = (bf16[24,21,512]{2,0,1:T(8,128)(2,1)S(1)}, bf16[24,21,512]{2,0,1:T(8,128)(2,1)S(1)}, u32[]{:S(2)}, u32[]{:S(2)}) collective-permute-start(bf16[24,21,512]{2,0,1:T(8,128)(2,1)S(1)} %copy.18), channel_id=1, source_target_pairs={{0,1},{1,2},{2,3},{4,5},{5,6},{6,7},{8,9},{9,10},{10,11},{12,13},{... | collective-permute-start | bytes 1548296 | tf_op jit(solution)/shard_map/ppermute | solution.py:23
  157.4 6.7 %collective-permute-start.14 = (bf16[21,66,512]{2,1,0:T(8,128)(2,1)S(1)}, bf16[21,66,512]{2,1,0:T(8,128)(2,1)S(1)}, u32[]{:S(2)}, u32[]{:S(2)}) collective-permute-start(bf16[21,66,512]{2,1,0:T(8,128)(2,1)S(1)} %get-tuple-element.15), channel_id=1, source_target_pairs={{0,4},{4,8},{8,12},{1,5},{5,9},{9,13},{2,6},{6,10},{10,14},{3,7},{... | collective-permute-start | bytes 4257800 | tf_op jit(solution)/shard_map/ppermute | solution.py:23
  161.2 5.7 %collective-permute-start.15 = (bf16[21,66,512]{2,1,0:T(8,128)(2,1)S(1)}, bf16[21,66,512]{2,1,0:T(8,128)(2,1)S(1)}, u32[]{:S(2)}, u32[]{:S(2)}) collective-permute-start(bf16[21,66,512]{2,1,0:T(8,128)(2,1)S(1)} %get-tuple-element.16), channel_id=1, source_target_pairs={{4,0},{8,4},{12,8},{5,1},{9,5},{13,9},{6,2},{10,6},{14,10},{7,3},{... | collective-permute-start | bytes 4257800 | tf_op jit(solution)/shard_map/ppermute | solution.py:25
  175.7 32.4 %copy-start.17 = (bf16[2048,256]{1,0:T(8,128)(2,1)S(1)}, bf16[2048,256]{1,0:T(8,128)(2,1)}, u32[]{:S(2)}) copy-start(bf16[2048,256]{1,0:T(8,128)(2,1)} %param.18) | copy-start | bytes 3145732
  175.7 6.7 %collective-permute-start.16 = (bf16[24,6,256]{2,1,0:T(8,128)(2,1)S(1)}, bf16[24,6,256]{2,1,0:T(8,128)(2,1)S(1)}, u32[]{:S(2)}, u32[]{:S(2)}) collective-permute-start(bf16[24,6,256]{2,1,0:T(8,128)(2,1)S(1)} %get-tuple-element.31), channel_id=1, source_target_pairs={{0,1},{1,2},{2,3},{4,5},{5,6},{6,7},{8,9},{9,10},{10,11},{12,13},{... | collective-permute-start | bytes 221192 | tf_op jit(solution)/shard_map/ppermute | solution.py:23
  180.3 6.5 %collective-permute-start.17 = (bf16[24,6,256]{2,1,0:T(8,128)(2,1)S(1)}, bf16[24,6,256]{2,1,0:T(8,128)(2,1)S(1)}, u32[]{:S(2)}, u32[]{:S(2)}) collective-permute-start(bf16[24,6,256]{2,1,0:T(8,128)(2,1)S(1)} %get-tuple-element.32), channel_id=1, source_target_pairs={{1,0},{2,1},{3,2},{5,4},{6,5},{7,6},{9,8},{10,9},{11,10},{13,12},{... | collective-permute-start | bytes 221192 | tf_op jit(solution)/shard_map/ppermute | solution.py:25
  186.9 19.9 %collective-permute-start.18 = (bf16[6,36,256]{2,1,0:T(8,128)(2,1)S(1)}, bf16[6,36,256]{2,1,0:T(8,128)(2,1)S(1)}, u32[]{:S(2)}, u32[]{:S(2)}) collective-permute-start(bf16[6,36,256]{2,1,0:T(8,128)(2,1)S(1)} %get-tuple-element.29), channel_id=1, source_target_pairs={{0,4},{4,8},{8,12},{1,5},{5,9},{9,13},{2,6},{6,10},{10,14},{3,7},{... | collective-permute-start | bytes 331784 | tf_op jit(solution)/shard_map/ppermute | solution.py:23
  204.3 3.7 collective-permute-start.19
  (15 other events, 108.7 us)
Sparse Core Ops, SparseCore 0:
  235.5 136.4 all-reduce.2

commit v2 on v1

--- a/solution.py
+++ b/solution.py
@@ -1,6 +1,10 @@
+import functools
+
 import jax
 import jax.numpy as jnp
 from jax import lax
+from jax.experimental import pallas as pl
+from jax.experimental.pallas import tpu as pltpu
 from jax.sharding import PartitionSpec as P
 
 LATER = 2
@@ -149,6 +153,163 @@
         "hwk,ck->hwc", projected_back, projection, preferred_element_type=jnp.float32
     )
     return section_back.astype(jnp.bfloat16)
+
+
+LANES = 256
+STREAMS = (("core", "section", "pair", "cols"), ("core", "pair", "section", "cols"))
+
+
+def total_kernel(sizes, x_ref, out_ref, acc, gathered, *rest):
+    steps = len(STREAMS[0])
+    sends = rest[: 2 * steps]
+    recvs = rest[2 * steps : 4 * steps]
+    send_sem, recv_sem = rest[4 * steps :]
+    row = lax.axis_index("rows")
+    place = {
+        "core": lax.rem(row, 2),
+        "pair": lax.div(row, 2),
+        "section": lax.axis_index("section"),
+        "cols": lax.axis_index("cols"),
+    }
+
+    def peer(stage, hop):
+        spot = dict(place)
+        spot[stage] = lax.rem(place[stage] + hop, sizes[stage])
+        return spot[stage], (spot["section"], spot["pair"] * 2 + spot["core"], spot["cols"])
+
+    barrier = pltpu.get_barrier_semaphore()
+    count = 0
+    for stage in STREAMS[0]:
+        for hop in range(1, sizes[stage]):
+            pl.semaphore_signal(
+                barrier, inc=1, device_id=peer(stage, hop)[1], device_id_type=pl.DeviceIdType.MESH
+            )
+            count += 1
+    pl.semaphore_wait(barrier, count)
+
+    half = x_ref.shape[0] // 2
+    starts = [0, half]
+    spans = [half, half]
+    history = [[], []]
+    for step in range(steps):
+        flying = []
+        source = x_ref if step == 0 else acc
+        for stream in range(2):
+            stage = STREAMS[stream][step]
+            parts = sizes[stage]
+            span = spans[stream] // parts
+            slot = 2 * step + stream
+            for hop in range(1, parts):
+                index, target = peer(stage, hop)
+                begin = pl.multiple_of(starts[stream] + index * span, 16)
+                sends[slot][hop - 1] = source[pl.ds(begin, span), :].astype(jnp.bfloat16)
+                copy = pltpu.make_async_remote_copy(
+                    src_ref=sends[slot].at[hop - 1],
+                    dst_ref=recvs[slot].at[hop - 1],
+                    send_sem=send_sem.at[slot, hop - 1],
+                    recv_sem=recv_sem.at[slot, hop - 1],
+                    device_id=target,
+                    device_id_type=pl.DeviceIdType.MESH,
+                )
+                copy.start()
+                flying.append(copy)
+        for copy in flying:
+            copy.wait()
+        for stream in range(2):
+            stage = STREAMS[stream][step]
+            parts = sizes[stage]
+            spans[stream] = spans[stream] // parts
+            starts[stream] = pl.multiple_of(
+                starts[stream] + place[stage] * spans[stream], 16
+            )
+            slot = 2 * step + stream
+            here = pl.ds(starts[stream], spans[stream])
+            summed = source[here, :]
+            for hop in range(1, parts):
+                summed = summed + recvs[slot][hop - 1].astype(jnp.float32)
+            acc[here, :] = summed
+            history[stream].append((starts[stream], spans[stream]))
+    for stream in range(2):
+        here = pl.ds(starts[stream], spans[stream])
+        gathered[here, :] = acc[here, :].astype(jnp.bfloat16)
+    for step in reversed(range(steps)):
+        flying = []
+        for stream in range(2):
+            stage = STREAMS[stream][step]
+            begin, span = history[stream][step]
+            slot = 2 * steps + 2 * step + stream
+            for hop in range(1, sizes[stage]):
+                block = gathered.at[pl.ds(begin, span), :]
+                copy = pltpu.make_async_remote_copy(
+                    src_ref=block,
+                    dst_ref=block,
+                    send_sem=send_sem.at[slot, hop - 1],
+                    recv_sem=recv_sem.at[slot, hop - 1],
+                    device_id=peer(stage, hop)[1],
+                    device_id_type=pl.DeviceIdType.MESH,
+                )
+                copy.start()
+                flying.append(copy)
+        for copy in flying:
+            copy.wait()
+    out_ref[...] = gathered[...].astype(jnp.float32)
+
+
+def total_over_devices(terms):
+    rows_count = lax.axis_size("rows")
+    sizes = {
+        "core": 2,
+        "pair": rows_count // 2,
+        "section": lax.axis_size("section"),
+        "cols": lax.axis_size("cols"),
+    }
+    length = terms.shape[0]
+    sends = []
+    for step in range(len(STREAMS[0])):
+        for stream in range(2):
+            span = length // 2
+            for stage in STREAMS[stream][: step + 1]:
+                span = span // sizes[stage]
+            parts = sizes[STREAMS[stream][step]]
+            sends.append(pltpu.VMEM((parts - 1, span, LANES), jnp.bfloat16))
+    slots = 4 * len(STREAMS[0])
+    most = max(sizes.values()) - 1
+    return pl.pallas_call(
+        functools.partial(total_kernel, sizes),
+        out_shape=jax.ShapeDtypeStruct(terms.shape, jnp.float32),
+        in_specs=[pl.BlockSpec(memory_space=pltpu.VMEM)],
+        out_specs=pl.BlockSpec(memory_space=pltpu.VMEM),
+        scratch_shapes=[
+            pltpu.VMEM(terms.shape, jnp.float32),
+            pltpu.VMEM(terms.shape, jnp.bfloat16),
+            *sends,
+            *sends,
+            pltpu.SemaphoreType.DMA((slots, most)),
+            pltpu.SemaphoreType.DMA((slots, most)),
+        ],
+        compiler_params=pltpu.CompilerParams(
+            collective_id=0, has_side_effects=True, vmem_limit_bytes=40 * 1024 * 1024
+        ),
+    )(terms)
+
+
+def total_gradients(grad_mid, grad_later):
+    devices = lax.axis_size("section") * lax.axis_size("rows") * lax.axis_size("cols")
+    channels = grad_mid.shape[0]
+    columns = -(-channels // LANES)
+    wide = jnp.pad(grad_mid, ((0, 0), (0, columns * LANES - channels)))
+    pieces = [wide[:, i * LANES : (i + 1) * LANES] for i in range(columns)]
+    pieces.append(grad_later.reshape(-1, LANES))
+    used = sum(piece.shape[0] for piece in pieces)
+    unit = 32 * devices
+    length = -(-used // unit) * unit
+    pieces.append(jnp.zeros((length - used, LANES), jnp.float32))
+    summed = total_over_devices(jnp.concatenate(pieces, axis=0))
+    wide = jnp.concatenate(
+        [summed[i * channels : (i + 1) * channels] for i in range(columns)], axis=1
+    )
+    later = summed[columns * channels : used].reshape(grad_later.shape)
+    return (wide[:, :channels], later)
 
 
 def local(
@@ -195,9 +356,7 @@
         section_back = head_end(padded_conv, depth_first, rate_first, projection)
         grad_mid = grad_mid + mid_gradient(mid_conv, section_back)
         grad_later = grad_later + later_terms
-    grad_later = lax.psum(grad_later, ("section", "rows", "cols"))
-    grad_mid = lax.psum(grad_mid, ("section", "rows", "cols"))
-    return (grad_mid, grad_later)
+    return total_gradients(grad_mid, grad_later)
 
 
 def solution(mesh):

time: 388 us -> 279 us (0.72)
  waiting for transfers between devices: 180 us -> 44.1 us
  Pallas kernels: 0 us -> 38.9 us
  between operations: 26.2 us -> 13.1 us
    psum x1 -> x0, waiting for transfers between devices: 137 us -> none  [local(): grad_mid = lax.psum(grad_mid, ('section', 'rows', 'cols'))]
    pallas_call x0 -> x1, Pallas kernels: none -> 38.9 us  [total_over_devices(): pl.pallas_call(functools.partial(total_kernel, sizes), out_shape=jax.Shap...]
  transfers between devices with their start and end apart: 21 -> 20, of which waited for: 15 -> 15; matrix products, arithmetic and copies ran while one was open for 1% -> 1% of each run, Pallas kernels for 0% -> 0%
where the time goes in v2:
time: 279 us; the launch traced here: 274 us
  starting transfers between devices  63.2 us (23%)
  matrix products  48.6 us (17%)
  waiting for transfers between devices  44.1 us (16%)
  Pallas kernels  38.9 us (14%)
  blocking collectives  34.8 us (12%)
  other arithmetic  18.7 us (7%)
  between operations  13.1 us (5%)
  local copies, waits for them, and re-layouts  12.4 us (4%)
    ppermute x10, starting transfers between devices, with_halo(): lax.ppermute(tail, axis, [(i, (i + 1) % count) for i in range(ends)])  49.7 us
    pallas_call x1, Pallas kernels, total_over_devices(): pl.pallas_call(functools.partial(total_kernel, sizes), out_shape=jax.Shap...  38.9 us
    ppermute x10, waiting for transfers between devices, with_halo(): lax.ppermute(head, axis, [((i + 1) % count, i) for i in range(ends)])  36.8 us
    all_to_all x1, blocking collectives, local(): tile = lax.all_to_all(slab, 'cols', split_axis=1, concat_axis=0, tiled=True)  34.8 us
    dot_general x1, matrix products, mid_gradient(): jnp.einsum('hwc,hwd->cd', mid_conv, section_back, preferred_element_type=...  23.3 us
    ppermute x10, starting transfers between devices, with_halo(): lax.ppermute(head, axis, [((i + 1) % count, i) for i in range(ends)])  13.5 us
    dot_general x1, matrix products, head_front(): jnp.einsum('hwc,cd->hwd', first_conv, point_first, preferred_element_type...  10.4 us
    concatenate x4, other arithmetic, with_halo(): jnp.concatenate([lax.ppermute(tail, axis, [(i, (i + 1) % count) for i in...  7.85 us
  transfers between devices with their start and end apart: 20, of which 15 were waited for; matrix products, arithmetic and copies ran while one was open for 1% of the time, Pallas kernels for 0%

profile of v2, /device:TPU:0, one launch (start us, length us, event | category | flops | bytes accessed | tf_op | source)
XLA Modules:
  0.0 273.8 jit_solution(13062984709200413957)
XLA Ops:
  2.5 34.8 %all_to_all.18 = bf16[6,96,728]{2,0,1:T(8,128)(2,1)S(1)} all-to-all(bf16[6,96,728]{2,0,1:T(8,128)(2,1)S(1)} %bitcast.119), channel_id=1, replica_groups=mesh['section'=2,'rows'=4,'cols'=4] {'cols'}, dimensions={1} | all-to-all | bytes 1677312 | tf_op jit(solution)/shard_map/all_to_all | solution.py:340
  41.7 4.3 %collective-permute-done.1 = bf16[24,1,728]{2,1,0:T(2,128)(2,1)S(1)} collective-permute-done((bf16[24,1,728]{2,1,0:T(2,128)(2,1)S(1)}, bf16[24,1,728]{2,1,0:T(2,128)(2,1)S(1)}, u32[]{:S(2)}, u32[]{:S(2)}) %collective-permute-start.1) | collective-permute-done | bytes 34976 | tf_op jit(solution)/shard_map/ppermute | solution.py:29
  48.7 3.5 %collective-permute-done.3 = bf16[1,26,728]{2,1,0:T(8,128)(2,1)S(1)} collective-permute-done((bf16[1,26,728]{2,1,0:T(8,128)(2,1)S(1)}, bf16[1,26,728]{2,1,0:T(8,128)(2,1)S(1)}, u32[]{:S(2)}, u32[]{:S(2)}) %collective-permute-start.3) | collective-permute-done | bytes 37888 | tf_op jit(solution)/shard_map/ppermute | solution.py:29
  57.7 2.5 collective-permute-start.4
  65.9 4.6 %collective-permute-done.5 = bf16[24,6,728]{2,1,0:T(8,128)(2,1)} collective-permute-done((bf16[24,6,728]{2,1,0:T(8,128)(2,1)}, bf16[24,6,728]{2,1,0:T(8,128)(2,1)}, u32[]{:S(2)}, u32[]{:S(2)}) %collective-permute-start.5) | collective-permute-done | bytes 209696 | tf_op jit(solution)/shard_map/ppermute | solution.py:29
  71.9 3.4 %collective-permute-start.6 = (bf16[6,36,728]{2,1,0:T(8,128)(2,1)S(1)}, bf16[6,36,728]{2,1,0:T(8,128)(2,1)S(1)}, u32[]{:S(2)}, u32[]{:S(2)}) collective-permute-start(bf16[6,36,728]{2,1,0:T(8,128)(2,1)S(1)} %get-tuple-element.18), channel_id=1, source_target_pairs={{0,4},{4,8},{8,12},{1,5},{5,9},{9,13},{2,6},{6,10},{10,14},{3,7},{... | collective-permute-start | bytes 943496 | tf_op jit(solution)/shard_map/ppermute | solution.py:27
  78.9 6.3 %convolution_convert_fusion = bf16[36,36,2048]{2,1,0:T(8,128)(2,1)S(1)} fusion(bf16[728,2048]{1,0:T(8,128)(2,1)S(1)} %copy-done, bf16[6,36,728]{2,1,0:T(8,128)(2,1)S(1)} %collective-permute-done.7, bf16[24,6,728]{2,1,0:T(8,128)(2,1)} %collective-permute-done.5, bf16[24,24,728]{2,1,0:T(8,128)(2,1)} %copy-done.2, ...), kind=kOutput, calls=%fused_computation.3 | convolution fusion | flops 3876615936 | bytes 10177280 | tf_op jit(solution)/shard_map/hwc,ck->hwk/dot_general | solution.py:82
  85.3 10.4 %multiply_convert_fusion = (bf16[24,24,256]{2,1,0:T(8,128)(2,1)S(1)}, f32[24,24,256]{2,1,0:T(8,128)}) fusion(bf16[2048,256]{1,0:T(8,128)(2,1)S(1)} %copy-done.19, bf16[36,36,2048]{2,1,0:T(8,128)(2,1)S(1)} %convolution_convert_fusion, f32[2048]{0:T(1024)S(1)} %bitcast.173, s32[]{:T(128)S(6)} %select_n.34, s32[]{:T(128)S(6)} %select_n.33, ...), kind=kOutput, calls=%fused_computation.94 | convolution fusion | flops 636567552 | bytes 23240720 | tf_op jit(solution)/shard_map/hwc,cd->hwd/dot_general | solution.py:93
  95.8 3.7 %collective-permute-start.8 = (bf16[24,21,256]{2,1,0:T(8,128)(2,1)S(1)}, bf16[24,21,256]{2,1,0:T(8,128)(2,1)S(1)}, u32[]{:S(2)}, u32[]{:S(2)}) collective-permute-start(bf16[24,21,256]{2,1,0:T(8,128)(2,1)S(1)} %get-tuple-element.34), channel_id=1, source_target_pairs={{0,1},{1,2},{2,3},{4,5},{5,6},{6,7},{8,9},{9,10},{10,11},{12,13},{... | collective-permute-start | bytes 774152 | tf_op jit(solution)/shard_map/ppermute | solution.py:27
  100.9 2.9 %collective-permute-done.8 = bf16[24,21,256]{2,1,0:T(8,128)(2,1)S(1)} collective-permute-done((bf16[24,21,256]{2,1,0:T(8,128)(2,1)S(1)}, bf16[24,21,256]{2,1,0:T(8,128)(2,1)S(1)}, u32[]{:S(2)}, u32[]{:S(2)}) %collective-permute-start.8) | collective-permute-done | bytes 258080 | tf_op jit(solution)/shard_map/ppermute | solution.py:27
  103.8 4.4 %collective-permute-done.9 = bf16[24,21,256]{2,1,0:T(8,128)(2,1)S(1)} collective-permute-done((bf16[24,21,256]{2,1,0:T(8,128)(2,1)S(1)}, bf16[24,21,256]{2,1,0:T(8,128)(2,1)S(1)}, u32[]{:S(2)}, u32[]{:S(2)}) %collective-permute-start.9) | collective-permute-done | bytes 258080 | tf_op jit(solution)/shard_map/ppermute | solution.py:29
  109.8 6.7 %collective-permute-start.10 = (bf16[21,66,256]{2,1,0:T(8,128)(2,1)}, bf16[21,66,256]{2,1,0:T(8,128)(2,1)}, u32[]{:S(2)}, u32[]{:S(2)}) collective-permute-start(bf16[21,66,256]{2,1,0:T(8,128)(2,1)} %get-tuple-element.22), channel_id=1, source_target_pairs={{0,4},{4,8},{8,12},{1,5},{5,9},{9,13},{2,6},{6,10},{10,14},{3,7},{... | collective-permute-start | bytes 2128904 | tf_op jit(solution)/shard_map/ppermute | solution.py:27
  135.2 4.6 %collective-permute-start.12 = (bf16[24,21,512]{2,0,1:T(8,128)(2,1)S(1)}, bf16[24,21,512]{2,0,1:T(8,128)(2,1)S(1)}, u32[]{:S(2)}, u32[]{:S(2)}) collective-permute-start(bf16[24,21,512]{2,0,1:T(8,128)(2,1)S(1)} %copy.18), channel_id=1, source_target_pairs={{0,1},{1,2},{2,3},{4,5},{5,6},{6,7},{8,9},{9,10},{10,11},{12,13},{... | collective-permute-start | bytes 1548296 | tf_op jit(solution)/shard_map/ppermute | solution.py:27
  139.8 8.9 %collective-permute-done.13 = bf16[24,21,512]{2,0,1:T(8,128)(2,1)S(1)} collective-permute-done((bf16[24,21,512]{2,0,1:T(8,128)(2,1)S(1)}, bf16[24,21,512]{2,0,1:T(8,128)(2,1)S(1)}, u32[]{:S(2)}, u32[]{:S(2)}) %collective-permute-start.13) | collective-permute-done | bytes 516128 | tf_op jit(solution)/shard_map/ppermute | solution.py:29
  151.6 3.4 %collective-permute-start.14 = (bf16[21,66,512]{2,1,0:T(8,128)(2,1)S(1)}, bf16[21,66,512]{2,1,0:T(8,128)(2,1)S(1)}, u32[]{:S(2)}, u32[]{:S(2)}) collective-permute-start(bf16[21,66,512]{2,1,0:T(8,128)(2,1)S(1)} %get-tuple-element.16), channel_id=1, source_target_pairs={{0,4},{4,8},{8,12},{1,5},{5,9},{9,13},{2,6},{6,10},{10,14},{3,7},{... | collective-permute-start | bytes 4257800 | tf_op jit(solution)/shard_map/ppermute | solution.py:27
  157.9 2.8 %collective-permute-done.15 = bf16[21,66,512]{2,1,0:T(8,128)(2,1)S(1)} collective-permute-done((bf16[21,66,512]{2,1,0:T(8,128)(2,1)S(1)}, bf16[21,66,512]{2,1,0:T(8,128)(2,1)S(1)}, u32[]{:S(2)}, u32[]{:S(2)}) %collective-permute-start.15) | collective-permute-done | bytes 1419296 | tf_op jit(solution)/shard_map/ppermute | solution.py:29
  160.7 5.3 %pad_maximum_fusion = bf16[66,66,512]{2,1,0:T(8,128)(2,1)S(1)} fusion(bf16[21,66,512]{2,1,0:T(8,128)(2,1)S(1)} %collective-permute-done.15, bf16[24,21,512]{2,1,0:T(8,128)(2,1)S(1)} %copy.21, bf16[24,24,256]{2,1,0:T(8,128)(2,1)S(1)} %convolution_convert_fusion.2, bf16[24,24,256]{2,1,0:T(8,128)(2,1)S(1)} %convolution_convert_fusion.3, ...), kind=kLoop, calls=%fused_computation | loop fusion | flops 26763264 | bytes 8921088 | tf_op jit(solution)/shard_map/concatenate | solution.py:25
  167.0 2.4 fusion.59
  169.4 4.5 %collective-permute-start.16 = (bf16[24,6,256]{2,1,0:T(8,128)(2,1)S(1)}, bf16[24,6,256]{2,1,0:T(8,128)(2,1)S(1)}, u32[]{:S(2)}, u32[]{:S(2)}) collective-permute-start(bf16[24,6,256]{2,1,0:T(8,128)(2,1)S(1)} %get-tuple-element.32), channel_id=1, source_target_pairs={{0,1},{1,2},{2,3},{4,5},{5,6},{6,7},{8,9},{9,10},{10,11},{12,13},{... | collective-permute-start | bytes 221192 | tf_op jit(solution)/shard_map/ppermute | solution.py:27
  176.1 4.3 %collective-permute-done.17 = bf16[24,6,256]{2,1,0:T(8,128)(2,1)S(1)} collective-permute-done((bf16[24,6,256]{2,1,0:T(8,128)(2,1)S(1)}, bf16[24,6,256]{2,1,0:T(8,128)(2,1)S(1)}, u32[]{:S(2)}, u32[]{:S(2)}) %collective-permute-start.17) | collective-permute-done | bytes 73760 | tf_op jit(solution)/shard_map/ppermute | solution.py:29
  180.6 17.5 %collective-permute-start.18 = (bf16[6,36,256]{2,1,0:T(8,128)(2,1)S(1)}, bf16[6,36,256]{2,1,0:T(8,128)(2,1)S(1)}, u32[]{:S(2)}, u32[]{:S(2)}) collective-permute-start(bf16[6,36,256]{2,1,0:T(8,128)(2,1)S(1)} %get-tuple-element.30), channel_id=1, source_target_pairs={{0,4},{4,8},{8,12},{1,5},{5,9},{9,13},{2,6},{6,10},{10,14},{3,7},{... | collective-permute-start | bytes 331784 | tf_op jit(solution)/shard_map/ppermute | solution.py:27
  201.7 4.3 %convolution_convert_fusion.1 = bf16[36,36,2048]{2,1,0:T(8,128)(2,1)} fusion(bf16[2048,256]{1,0:T(8,128)(2,1)S(1)} %copy-done.20, bf16[6,36,256]{2,1,0:T(8,128)(2,1)S(1)} %collective-permute-done.19, bf16[24,6,256]{2,1,0:T(8,128)(2,1)S(1)} %collective-permute-done.17, bf16[24,24,256]{2,1,0:T(8,128)(2,1)S(1)} %fusion.59, ...), kind=kOutput, calls=%fused_computation.4 | convolution fusion | flops 1364926464 | bytes 7020544 | tf_op jit(solution)/shard_map/hwd,cd->hwc/dot_general | solution.py:141
  206.1 23.3 %convolution_bitcast_fusion = f32[728,728]{1,0:T(8,128)} fusion(bf16[24,24,728]{2,1,0:T(8,128)(2,1)} %copy-done.7, bf16[728,2048]{1,0:T(8,128)(2,1)S(1)} %copy-done, bf16[36,36,2048]{2,1,0:T(8,128)(2,1)} %convolution_convert_fusion.1, s32[]{:T(128)S(6)} %select_n.31, s32[]{:T(128)S(6)} %select_n.32, s32[]{:T(128)S(6)} %select_n.33, s32[]{:T(128)S(6)} %select_n.34, ...), kind=kOutput, calls=%fused_computation.47 | convolution fusion | flops 2360378880 | bytes 27293968 | tf_op jit(solution)/shard_map/hwc,hwd->cd/dot_general | solution.py:78
  232.0 38.9 %shard_map.131 = f32[3072,256]{1,0:T(8,128)S(1)} custom-call(f32[3072,256]{1,0:T(8,128)S(1)} %broadcast_dynamic-update-slice_fusion.x_ref), custom_call_target="tpu_custom_call" | custom-call | tf_op jit(solution)/shard_map/pallas_call | solution.py:277
  (113 shorter events, 53.2 us)
Async XLA Ops:
  0.6 78.3 %copy-start = (bf16[728,2048]{1,0:T(8,128)(2,1)S(1)}, bf16[728,2048]{1,0:T(8,128)(2,1)}, u32[]{:S(2)}) copy-start(bf16[728,2048]{1,0:T(8,128)(2,1)} %param.16) | copy-start | bytes 8945668
  2.5 46.1 %copy-start.12 = (f32[9,728]{1,0:T(8,128)S(1)}, f32[9,728]{1,0:T(8,128)}, u32[]{:S(2)}) copy-start(f32[9,728]{1,0:T(8,128)} %param.14) | copy-start | bytes 78628
  37.6 4.1 %collective-permute-start = (bf16[24,1,728]{2,1,0:T(2,128)(2,1)S(1)}, bf16[24,1,728]{2,1,0:T(2,128)(2,1)S(1)}, u32[]{:S(2)}, u32[]{:S(2)}) collective-permute-start(bf16[24,1,728]{2,1,0:T(2,128)(2,1)S(1)} %get-tuple-element.26), channel_id=1, source_target_pairs={{0,1},{1,2},{2,3},{4,5},{5,6},{6,7},{8,9},{9,10},{10,11},{12,13},{... | collective-permute-start | bytes 104840 | tf_op jit(solution)/shard_map/ppermute | solution.py:27
  39.7 6.2 %collective-permute-start.1 = (bf16[24,1,728]{2,1,0:T(2,128)(2,1)S(1)}, bf16[24,1,728]{2,1,0:T(2,128)(2,1)S(1)}, u32[]{:S(2)}, u32[]{:S(2)}) collective-permute-start(bf16[24,1,728]{2,1,0:T(2,128)(2,1)S(1)} %get-tuple-element.27), channel_id=1, source_target_pairs={{1,0},{2,1},{3,2},{5,4},{6,5},{7,6},{9,8},{10,9},{11,10},{13,12},{... | collective-permute-start | bytes 104840 | tf_op jit(solution)/shard_map/ppermute | solution.py:29
  46.0 2.7 collective-permute-start.2
  47.3 4.9 %collective-permute-start.3 = (bf16[1,26,728]{2,1,0:T(8,128)(2,1)S(1)}, bf16[1,26,728]{2,1,0:T(8,128)(2,1)S(1)}, u32[]{:S(2)}, u32[]{:S(2)}) collective-permute-start(bf16[1,26,728]{2,1,0:T(8,128)(2,1)S(1)} %get-tuple-element.21), channel_id=1, source_target_pairs={{4,0},{8,4},{12,8},{5,1},{9,5},{13,9},{6,2},{10,6},{14,10},{7,3},{... | collective-permute-start | bytes 113576 | tf_op jit(solution)/shard_map/ppermute | solution.py:29
  57.7 8.3 %collective-permute-start.4 = (bf16[24,6,728]{2,1,0:T(8,128)(2,1)}, bf16[24,6,728]{2,1,0:T(8,128)(2,1)S(1)}, u32[]{:S(2)}, u32[]{:S(2)}) collective-permute-start(bf16[24,6,728]{2,1,0:T(8,128)(2,1)} %get-tuple-element.24), channel_id=1, source_target_pairs={{0,1},{1,2},{2,3},{4,5},{5,6},{6,7},{8,9},{9,10},{10,11},{12,13},{... | collective-permute-start | bytes 629000 | tf_op jit(solution)/shard_map/ppermute | solution.py:27
  60.1 10.4 %collective-permute-start.5 = (bf16[24,6,728]{2,1,0:T(8,128)(2,1)}, bf16[24,6,728]{2,1,0:T(8,128)(2,1)}, u32[]{:S(2)}, u32[]{:S(2)}) collective-permute-start(bf16[24,6,728]{2,1,0:T(8,128)(2,1)} %get-tuple-element.25), channel_id=1, source_target_pairs={{1,0},{2,1},{3,2},{5,4},{6,5},{7,6},{9,8},{10,9},{11,10},{13,12},{... | collective-permute-start | bytes 629000 | tf_op jit(solution)/shard_map/ppermute | solution.py:29
  71.9 5.0 %collective-permute-start.6 = (bf16[6,36,728]{2,1,0:T(8,128)(2,1)S(1)}, bf16[6,36,728]{2,1,0:T(8,128)(2,1)S(1)}, u32[]{:S(2)}, u32[]{:S(2)}) collective-permute-start(bf16[6,36,728]{2,1,0:T(8,128)(2,1)S(1)} %get-tuple-element.18), channel_id=1, source_target_pairs={{0,4},{4,8},{8,12},{1,5},{5,9},{9,13},{2,6},{6,10},{10,14},{3,7},{... | collective-permute-start | bytes 943496 | tf_op jit(solution)/shard_map/ppermute | solution.py:27
  75.3 3.6 %collective-permute-start.7 = (bf16[6,36,728]{2,1,0:T(8,128)(2,1)S(1)}, bf16[6,36,728]{2,1,0:T(8,128)(2,1)S(1)}, u32[]{:S(2)}, u32[]{:S(2)}) collective-permute-start(bf16[6,36,728]{2,1,0:T(8,128)(2,1)S(1)} %get-tuple-element.19), channel_id=1, source_target_pairs={{4,0},{8,4},{12,8},{5,1},{9,5},{13,9},{6,2},{10,6},{14,10},{7,3},{... | collective-permute-start | bytes 943496 | tf_op jit(solution)/shard_map/ppermute | solution.py:29
  95.8 30.2 %copy-start.11 = (f32[2,9,256]{2,0,1:T(2,128)S(1)}, f32[2,9,256]{2,0,1:T(2,128)}, u32[]{:S(2)}) copy-start(f32[2,9,256]{2,0,1:T(2,128)} %param.19) | copy-start | bytes 55300
  95.8 7.9 %collective-permute-start.8 = (bf16[24,21,256]{2,1,0:T(8,128)(2,1)S(1)}, bf16[24,21,256]{2,1,0:T(8,128)(2,1)S(1)}, u32[]{:S(2)}, u32[]{:S(2)}) collective-permute-start(bf16[24,21,256]{2,1,0:T(8,128)(2,1)S(1)} %get-tuple-element.34), channel_id=1, source_target_pairs={{0,1},{1,2},{2,3},{4,5},{5,6},{6,7},{8,9},{9,10},{10,11},{12,13},{... | collective-permute-start | bytes 774152 | tf_op jit(solution)/shard_map/ppermute | solution.py:27
  99.6 8.6 %collective-permute-start.9 = (bf16[24,21,256]{2,1,0:T(8,128)(2,1)S(1)}, bf16[24,21,256]{2,1,0:T(8,128)(2,1)S(1)}, u32[]{:S(2)}, u32[]{:S(2)}) collective-permute-start(bf16[24,21,256]{2,1,0:T(8,128)(2,1)S(1)} %get-tuple-element.35), channel_id=1, source_target_pairs={{1,0},{2,1},{3,2},{5,4},{6,5},{7,6},{9,8},{10,9},{11,10},{13,12},{... | collective-permute-start | bytes 774152 | tf_op jit(solution)/shard_map/ppermute | solution.py:29
  109.8 17.9 %collective-permute-start.10 = (bf16[21,66,256]{2,1,0:T(8,128)(2,1)}, bf16[21,66,256]{2,1,0:T(8,128)(2,1)}, u32[]{:S(2)}, u32[]{:S(2)}) collective-permute-start(bf16[21,66,256]{2,1,0:T(8,128)(2,1)} %get-tuple-element.22), channel_id=1, source_target_pairs={{0,4},{4,8},{8,12},{1,5},{5,9},{9,13},{2,6},{6,10},{10,14},{3,7},{... | collective-permute-start | bytes 2128904 | tf_op jit(solution)/shard_map/ppermute | solution.py:27
  116.4 11.3 %collective-permute-start.11 = (bf16[21,66,256]{2,1,0:T(8,128)(2,1)}, bf16[21,66,256]{2,1,0:T(8,128)(2,1)}, u32[]{:S(2)}, u32[]{:S(2)}) collective-permute-start(bf16[21,66,256]{2,1,0:T(8,128)(2,1)} %get-tuple-element.23), channel_id=1, source_target_pairs={{4,0},{8,4},{12,8},{5,1},{9,5},{13,9},{6,2},{10,6},{14,10},{7,3},{... | collective-permute-start | bytes 2128904 | tf_op jit(solution)/shard_map/ppermute | solution.py:29
  133.7 14.9 %collective-permute-start.13 = (bf16[24,21,512]{2,0,1:T(8,128)(2,1)S(1)}, bf16[24,21,512]{2,0,1:T(8,128)(2,1)S(1)}, u32[]{:S(2)}, u32[]{:S(2)}) collective-permute-start(bf16[24,21,512]{2,0,1:T(8,128)(2,1)S(1)} %copy.19), channel_id=1, source_target_pairs={{1,0},{2,1},{3,2},{5,4},{6,5},{7,6},{9,8},{10,9},{11,10},{13,12},{... | collective-permute-start | bytes 1548296 | tf_op jit(solution)/shard_map/ppermute | solution.py:29
  135.2 15.4 %collective-permute-start.12 = (bf16[24,21,512]{2,0,1:T(8,128)(2,1)S(1)}, bf16[24,21,512]{2,0,1:T(8,128)(2,1)S(1)}, u32[]{:S(2)}, u32[]{:S(2)}) collective-permute-start(bf16[24,21,512]{2,0,1:T(8,128)(2,1)S(1)} %copy.18), channel_id=1, source_target_pairs={{0,1},{1,2},{2,3},{4,5},{5,6},{6,7},{8,9},{9,10},{10,11},{12,13},{... | collective-permute-start | bytes 1548296 | tf_op jit(solution)/shard_map/ppermute | solution.py:27
  151.6 6.3 %collective-permute-start.14 = (bf16[21,66,512]{2,1,0:T(8,128)(2,1)S(1)}, bf16[21,66,512]{2,1,0:T(8,128)(2,1)S(1)}, u32[]{:S(2)}, u32[]{:S(2)}) collective-permute-start(bf16[21,66,512]{2,1,0:T(8,128)(2,1)S(1)} %get-tuple-element.16), channel_id=1, source_target_pairs={{0,4},{4,8},{8,12},{1,5},{5,9},{9,13},{2,6},{6,10},{10,14},{3,7},{... | collective-permute-start | bytes 4257800 | tf_op jit(solution)/shard_map/ppermute | solution.py:27
  155.0 5.6 %collective-permute-start.15 = (bf16[21,66,512]{2,1,0:T(8,128)(2,1)S(1)}, bf16[21,66,512]{2,1,0:T(8,128)(2,1)S(1)}, u32[]{:S(2)}, u32[]{:S(2)}) collective-permute-start(bf16[21,66,512]{2,1,0:T(8,128)(2,1)S(1)} %get-tuple-element.17), channel_id=1, source_target_pairs={{4,0},{8,4},{12,8},{5,1},{9,5},{13,9},{6,2},{10,6},{14,10},{7,3},{... | collective-permute-start | bytes 4257800 | tf_op jit(solution)/shard_map/ppermute | solution.py:29
  169.4 32.4 %copy-start.20 = (bf16[2048,256]{1,0:T(8,128)(2,1)S(1)}, bf16[2048,256]{1,0:T(8,128)(2,1)}, u32[]{:S(2)}) copy-start(bf16[2048,256]{1,0:T(8,128)(2,1)} %param.18) | copy-start | bytes 3145732
  169.4 6.7 %collective-permute-start.16 = (bf16[24,6,256]{2,1,0:T(8,128)(2,1)S(1)}, bf16[24,6,256]{2,1,0:T(8,128)(2,1)S(1)}, u32[]{:S(2)}, u32[]{:S(2)}) collective-permute-start(bf16[24,6,256]{2,1,0:T(8,128)(2,1)S(1)} %get-tuple-element.32), channel_id=1, source_target_pairs={{0,1},{1,2},{2,3},{4,5},{5,6},{6,7},{8,9},{9,10},{10,11},{12,13},{... | collective-permute-start | bytes 221192 | tf_op jit(solution)/shard_map/ppermute | solution.py:27
  174.0 6.5 %collective-permute-start.17 = (bf16[24,6,256]{2,1,0:T(8,128)(2,1)S(1)}, bf16[24,6,256]{2,1,0:T(8,128)(2,1)S(1)}, u32[]{:S(2)}, u32[]{:S(2)}) collective-permute-start(bf16[24,6,256]{2,1,0:T(8,128)(2,1)S(1)} %get-tuple-element.33), channel_id=1, source_target_pairs={{1,0},{2,1},{3,2},{5,4},{6,5},{7,6},{9,8},{10,9},{11,10},{13,12},{... | collective-permute-start | bytes 221192 | tf_op jit(solution)/shard_map/ppermute | solution.py:29
  180.6 19.1 %collective-permute-start.18 = (bf16[6,36,256]{2,1,0:T(8,128)(2,1)S(1)}, bf16[6,36,256]{2,1,0:T(8,128)(2,1)S(1)}, u32[]{:S(2)}, u32[]{:S(2)}) collective-permute-start(bf16[6,36,256]{2,1,0:T(8,128)(2,1)S(1)} %get-tuple-element.30), channel_id=1, source_target_pairs={{0,4},{4,8},{8,12},{1,5},{5,9},{9,13},{2,6},{6,10},{10,14},{3,7},{... | collective-permute-start | bytes 331784 | tf_op jit(solution)/shard_map/ppermute | solution.py:27
  198.0 3.7 %collective-permute-start.19 = (bf16[6,36,256]{2,1,0:T(8,128)(2,1)S(1)}, bf16[6,36,256]{2,1,0:T(8,128)(2,1)S(1)}, u32[]{:S(2)}, u32[]{:S(2)}) collective-permute-start(bf16[6,36,256]{2,1,0:T(8,128)(2,1)S(1)} %get-tuple-element.31), channel_id=1, source_target_pairs={{4,0},{8,4},{12,8},{5,1},{9,5},{13,9},{6,2},{10,6},{14,10},{7,3},{... | collective-permute-start | bytes 331784 | tf_op jit(solution)/shard_map/ppermute | solution.py:29
  (17 other events, 103.2 us)
